TPU v7x, 256 devices: a whole 4x4x8 slice. The times are simulated.
256 devices in a mesh: fluid: 8 (over z), inflow: 8 (over y, core), solid: 4 (over x).
Axes of the slice: x: 4, y: 4, z: 8, core: 2. Of those that a mesh axis runs over, the one named last changes fastest.
Arguments:
- state: float32 [4, 4, 32, 128, 1024], P('solid', None, None, 'fluid', 'inflow'), may hold values from -5 to 5
- precursor: bfloat16 [4, 2, 4, 131072], P('solid', None, None, ('fluid', 'inflow')), may hold values from -5 to 5
- inlet_map: int32 [4, 128, 1024], P('solid', 'fluid', 'inflow'), may hold values from 0 to 131071, as said below
- face_cell: int32 [4, 8, 8, 4096], P('solid', 'fluid', 'inflow'), may hold values from 0 to 65535
- face_owner: int32 [4, 8, 8, 4096, 1], P('solid', 'fluid', 'inflow'), may hold values from 0 to 3; in each aligned block of 4096 rows (0 to 4095, 4096 to 8191, ..., all dimensions but the last counted through in order) at most 2048 rows name the same one
- wall_temp: float32 [4, 8, 8, 8, 8192], P('solid', 'fluid', 'inflow'), may hold values from -4 to 4
Outputs:
- new_state: float32 [4, 4, 32, 128, 1024], P('solid', None, None, 'fluid', 'inflow')
- new_wall: float32 [4, 8, 8, 8, 8192], P('solid', 'fluid', 'inflow')
Inputs may be any that keep to these rules, and one draw needn't show every extreme that they name: `inlet_map`: for each runner and each block of 16 rows, the block's entries are a permutation of the precursor cells whose row (value // 1024) lies in the same block. `face_cell`: Device-local cell indices; cells may repeat. `face_owner`: in the rows of one device no owner is named by more than 2048 faces; some device names one owner exactly 2048 times.
All inputs are finite; a program needn't handle non-finite values.
Results may differ from a plain program's by a relative error of at most 0.0003.
Values may be sent and summed in bfloat16 or wider, within the bound.
A program may use at most 128 MiB of HBM per device.

v0:
```python
import jax
import jax.numpy as jnp
from jax import lax
from jax.sharding import PartitionSpec as P

STEPS = 2
CAP = 2048


TIME_STEP = 0.1
VISCOSITY = 0.5
HEAT_TRANSFER = 0.8
CONDUCT_SLOPE = 0.2
SOLID_STEP = 0.15
WALL_WEIGHT = 0.5


def extended(shard, sides, width):
    for axis, dim in sides:
        devices, length = (lax.axis_size(axis), shard.shape[dim])
        up = [(i, (i + 1) % devices) for i in range(devices - 1)]
        down = [(j, i) for i, j in up]
        last = lax.slice_in_dim(shard, length - width, length, axis=dim)
        initial = lax.slice_in_dim(shard, 0, width, axis=dim)
        before = lax.ppermute(last, axis, up)
        after = lax.ppermute(initial, axis, down)
        shard = jnp.concatenate([before, shard, after], axis=dim)
    return shard


def update(flow_field, minus_x, plus_x, minus_y, plus_y, minus_z, plus_z, heat_term):
    laplace = minus_x + plus_x + minus_y + plus_y + minus_z + plus_z - 6.0 * flow_field
    advection = 0.5 * (
        flow_field[0:1] * (plus_x - minus_x)
        + flow_field[1:2] * (plus_y - minus_y)
        + flow_field[2:3] * (plus_z - minus_z)
    )
    updated = flow_field + TIME_STEP * (VISCOSITY * laplace - advection)
    return updated.at[3].add(heat_term)


def conduct(received, valid_in, solid_temps):
    speed_sq = received[..., 0, :] ** 2 + received[..., 1, :] ** 2 + received[..., 2, :] ** 2
    transfer = HEAT_TRANSFER * (1.0 + 0.5 * speed_sq)
    wall_flux = valid_in * transfer * (received[..., 3, :] - solid_temps[..., 0, :])
    conductivity = jnp.exp(CONDUCT_SLOPE * solid_temps)
    interface = (
        0.5
        * (conductivity[..., :-1, :] + conductivity[..., 1:, :])
        * (solid_temps[..., 1:, :] - solid_temps[..., :-1, :])
    )
    outermost = conductivity[..., -1:, :] * (0.0 - solid_temps[..., -1:, :])
    from_above = jnp.concatenate([interface, outermost], axis=-2)
    from_below = jnp.concatenate([wall_flux[..., None, :], -interface], axis=-2)
    return (wall_flux, solid_temps + SOLID_STEP * (from_above + from_below))


def inlet_planes(window, relative, across, upward):
    taken = jnp.take(window, relative, axis=2).astype(jnp.float32)
    return taken.reshape(window.shape[0], window.shape[1], across, upward)


def advance(flow_field, inlet_plane, heat_term):
    padded = extended(flow_field, (("fluid", 2), ("inflow", 3)), 1)
    minus_x = jnp.concatenate([inlet_plane[:, None], flow_field[:, :-1]], axis=1)
    plus_x = jnp.concatenate([flow_field[:, 1:], flow_field[:, -1:]], axis=1)
    return update(
        flow_field,
        minus_x,
        plus_x,
        padded[:, :, :-2, 1:-1],
        padded[:, :, 2:, 1:-1],
        padded[:, :, 1:-1, :-2],
        padded[:, :, 1:-1, 2:],
        heat_term,
    )


def local(state, precursor, inlet_map, face_cell, face_owner, wall_temp):
    flow_field = state[0]
    components, streamwise, across, upward = flow_field.shape
    cell_total = streamwise * across * upward
    solid_count = lax.axis_size("solid")
    block_cells = across * upward * lax.axis_size("inflow")
    relative = (inlet_map[0] - lax.axis_index("fluid") * block_cells).reshape(-1)
    wall_cells = face_cell[0, 0, 0]
    face_owners = face_owner[0, 0, 0, :, 0]
    columns = solid_count * CAP
    solid_temps = wall_temp[0, 0, 0]
    choose = (face_owners[:, None] == jnp.arange(solid_count, dtype=jnp.int32)[None, :]).astype(
        jnp.int32
    )
    face_rank = jnp.sum(choose * (jnp.cumsum(choose, axis=0) - 1), axis=1)
    slot_index = face_owners * CAP + face_rank
    valid_slots = jnp.zeros((columns,), jnp.float32).at[slot_index].set(1.0)
    slot_cell = jnp.zeros((columns,), jnp.int32).at[slot_index].set(wall_cells)
    valid_out = valid_slots.reshape(1, solid_count, CAP)
    for step_index in range(STEPS):
        window = lax.all_gather(
            precursor[:, step_index : step_index + 1], "inflow", axis=3, tiled=True
        )
        inlet_plane = inlet_planes(window[0], relative, across, upward)[0]
        flat_field = flow_field.reshape(components, -1)
        send_buffer = flat_field[:, slot_cell] * valid_slots[None, :]
        received, slot_marks = (
            lax.all_to_all(
                send_buffer.reshape(components, solid_count, CAP),
                "solid",
                split_axis=1,
                concat_axis=1,
                tiled=True,
            ),
            lax.all_to_all(valid_out, "solid", split_axis=1, concat_axis=1, tiled=True),
        )
        wall_flux, solid_temps = conduct(
            received.reshape(components, columns), slot_marks.reshape(columns), solid_temps
        )
        returned = lax.all_to_all(
            wall_flux.reshape(solid_count, CAP), "solid", split_axis=0, concat_axis=0, tiled=True
        )
        heat_term = (
            jnp.zeros((cell_total,), jnp.float32)
            .at[slot_cell]
            .add(-WALL_WEIGHT * returned.reshape(-1) * valid_slots)
        )
        flow_field = advance(flow_field, inlet_plane, heat_term.reshape(streamwise, across, upward))
    return (flow_field[None], solid_temps[None, None, None])


def solution(mesh):
    return jax.shard_map(
        local,
        mesh=mesh,
        in_specs=(
            P("solid", None, None, "fluid", "inflow"),
            P("solid", None, None, ("fluid", "inflow")),
            P("solid", "fluid", "inflow"),
            P("solid", "fluid", "inflow", None),
            P("solid", "fluid", "inflow", None, None),
            P("solid", "fluid", "inflow", None, None),
        ),
        out_specs=(
            P("solid", None, None, "fluid", "inflow"),
            P("solid", "fluid", "inflow", None, None),
        ),
        check_vma=False,
    )
```

profile of v0, /device:TPU:1, one launch (start us, length us, event | category | flops | bytes accessed | tf_op | source)
XLA Modules:
  0.0 437.1 jit_solution(6612603128098227346)
XLA Ops:
  1.4 1.1 reduce-window.6
  4.6 16.1 %scatter_custom_fusion.1 = f32[8192]{0:T(1024)} fusion(s32[4096]{0:T(1024)S(1)} %bitcast.157, f32[4096]{0:T(1024)S(1)} %broadcast.354, f32[]{:T(128)} %constant.95.clone.1), kind=kCustom, calls=%fused_computation.118 | custom fusion | bytes 32772 | tf_op jit(solution)/shard_map/scatter | solution.py:95
  21.5 15.7 %scatter_custom_fusion = s32[8192]{0:T(1024)S(1)} fusion(s32[4096]{0:T(1024)S(1)} %bitcast.158, s32[4096]{0:T(1024)} %bitcast.160, s32[]{:T(128)} %constant.96.clone.1), kind=kCustom, calls=%fused_computation.120 | custom fusion | bytes 33280 | tf_op jit(solution)/shard_map/scatter | solution.py:96
  37.8 17.5 %copy.58 = f32[1,4,32,16,128]{1,4,3,2,0:T(8,128)} copy(f32[1,4,32,16,128]{4,3,2,1,0:T(8,128)} %param.12) | data formatting | bytes 2097152 | tf_op args[0]
  55.4 38.4 %gather_fusion = f32[8192,4]{1,0:T(8,128)} fusion(f32[4,65536]{0,1:T(8,128)} %bitcast.132, s32[8192]{0:T(1024)S(1)} %get-tuple-element.71), kind=kCustom, calls=%fused_computation.2 | custom fusion | bytes 294912 | tf_op jit(solution)/shard_map/gather | solution.py:104
  93.8 2.9 copy.59
  97.4 4.8 %all-to-all-start.1 = ((f32[4,4,2048]{2,0,1:T(4,128)}), f32[4,4,2048]{2,0,1:T(4,128)S(1)}, u32[]{:S(2)}, u32[]{:S(2)}) async-start(f32[4,4,2048]{2,0,1:T(4,128)} %broadcast_multiply_fusion.1), calls=%async_computation.1 | async-start | bytes 262144 | tf_op jit(solution)/shard_map/all_to_all | solution.py:106
  103.0 4.2 collective-permute-start
  107.1 1.3 collective-permute-start.1
  108.5 1.5 fusion.53
  111.2 24.8 %all_gather.6 = bf16[1,1,4,16384]{2,3,1,0:T(8,128)(2,1)} all-gather(bf16[1,1,4,2048]{2,3,1,0:T(8,128)(2,1)S(1)} %copy.80), channel_id=1, replica_groups=mesh['fluid'=8,'inflow'=8,'solid'=4] {'inflow'}, dimensions={3}, use_global_device_ids=true | all-gather | bytes 147456 | tf_op jit(solution)/shard_map/all_gather | solution.py:99
  136.3 23.1 %all_gather.7 = bf16[1,1,4,16384]{2,3,1,0:T(8,128)(2,1)} all-gather(bf16[1,1,4,2048]{2,3,1,0:T(8,128)(2,1)S(1)} %copy.84), channel_id=1, replica_groups=mesh['fluid'=8,'inflow'=8,'solid'=4] {'inflow'}, dimensions={3}, use_global_device_ids=true | all-gather | bytes 147456 | tf_op jit(solution)/shard_map/all_gather | solution.py:99
  159.4 10.4 %gather_fusion.2 = bf16[2048,4]{1,0:T(8,128)(2,1)} fusion(bf16[4,16384]{0,1:T(8,128)(2,1)} %bitcast.134, s32[2048]{0:T(1024)S(1)} %fusion.43), kind=kCustom, calls=%fused_computation.clone | custom fusion | bytes 40960 | tf_op jit(solution)/shard_map/jit(_take)/gather | solution.py:59
  169.9 10.4 %gather_fusion.3 = bf16[2048,4]{1,0:T(8,128)(2,1)} fusion(bf16[4,16384]{0,1:T(8,128)(2,1)} %bitcast.135, s32[2048]{0:T(1024)S(1)} %fusion.43), kind=kCustom, calls=%fused_computation.1.clone | custom fusion | bytes 40960 | tf_op jit(solution)/shard_map/jit(_take)/gather | solution.py:59
  180.3 1.5 bitcast_select_fusion
  183.7 2.2 fusion.50
  185.8 2.5 copy.54
  188.4 1.9 collective-permute-start.2
  190.3 2.5 copy.56
  192.8 3.0 collective-permute-start.3
  197.1 1.4 squeeze.47
  200.8 2.6 copy.55
  203.4 2.5 copy.57
  205.9 3.8 multiply_add_fusion.1
  209.7 4.5 %all-to-all-start = ((f32[1,4,2048]{2,0,1:T(1,128)}), f32[1,4,2048]{2,0,1:T(1,128)S(1)}, u32[]{:S(2)}, u32[]{:S(2)}) async-start(f32[1,4,2048]{2,0,1:T(1,128)} %bitcast.17), calls=%async_computation | async-start | bytes 65536 | tf_op jit(solution)/shard_map/all_to_all | solution.py:113
  214.3 4.3 all-to-all-done
  220.1 3.4 all-to-all-start.2
  223.7 1.1 multiply_exponential_fusion
  228.5 50.3 %scatter_custom_fusion.2 = f32[65536]{0:T(1024)S(1)} fusion(s32[8192]{0:T(1024)} %get-tuple-element.72, f32[8192]{0:T(1024)S(1)} %mul.403, f32[]{:T(128)} %constant.95.clone.1), kind=kCustom, calls=%fused_computation.67 | custom fusion | flops 8192 | bytes 262656 | tf_op jit(solution)/shard_map/scatter-add | solution.py:124
  278.9 16.6 %copy.71 = f32[4,32,16,128]{0,3,2,1:T(8,128)} copy(f32[4,32,16,128]{3,2,1,0:T(8,128)S(1)} %fusion.6) | data formatting | bytes 2097152 | tf_op jit(solution)/shard_map/scatter-add | solution.py:39
  295.6 38.4 %gather_fusion.1 = f32[8192,4]{1,0:T(8,128)} fusion(f32[4,65536]{0,1:T(8,128)} %bitcast.131, s32[8192]{0:T(1024)S(1)} %copy-done.9), kind=kCustom, calls=%fused_computation.3 | custom fusion | bytes 294912 | tf_op jit(solution)/shard_map/gather | solution.py:104
  334.0 2.8 copy.72
  337.5 3.9 collective-permute-start.4
  341.5 1.3 collective-permute-start.5
  342.8 1.5 fusion.51
  344.2 2.2 collective-permute-done.5
  347.3 1.7 fusion.49
  349.0 2.5 copy.67
  351.5 6.5 %collective-permute-start.6 = (f32[4,32,18,1]{1,0,3,2:T(4,128)}, f32[4,32,18,1]{1,0,3,2:T(4,128)}, u32[]{:S(2)}, u32[]{:S(2)}) collective-permute-start(f32[4,32,18,1]{1,0,3,2:T(4,128)} %copy.67), channel_id=1, source_target_pairs={{0,4},{4,8},{8,12},{12,16},{16,20},{20,24},{24,28},{1,5},{5,9},{9,... | collective-permute-start | bytes 27656 | tf_op jit(solution)/shard_map/ppermute | solution.py:25
  358.0 1.1 copy.69
  359.2 1.9 collective-permute-start.7
  362.6 3.3 all-to-all-start.3
  365.9 1.4 copy.68
  367.3 2.6 copy.70
  369.9 3.6 multiply_add_fusion
  375.5 4.2 all-to-all-start.4
  381.7 2.3 all-to-all-done.4
  384.8 50.3 %scatter_custom_fusion.3 = f32[65536]{0:T(1024)S(1)} fusion(s32[8192]{0:T(1024)} %get-tuple-element.72, f32[8192]{0:T(1024)S(1)} %mul.434, f32[]{:T(128)} %constant.95.clone.1), kind=kCustom, calls=%fused_computation.65 | custom fusion | flops 8192 | bytes 262656 | tf_op jit(solution)/shard_map/scatter-add | solution.py:124
  (107 shorter events, 27.9 us)
Async XLA Ops:
  21.5 75.2 %copy-start.10 = (f32[4,2048]{1,0:T(4,128)}, f32[4,2048]{1,0:T(4,128)S(1)}, u32[]{:S(2)}) copy-start(f32[4,2048]{1,0:T(4,128)S(1)} %mul.393) | copy-start | bytes 98308
  37.8 17.6 %copy-start.8 = (s32[8192]{0:T(1024)}, s32[8192]{0:T(1024)S(1)}, u32[]{:S(2)}) copy-start(s32[8192]{0:T(1024)S(1)} %get-tuple-element.71) | copy-start | bytes 98308
  93.8 8.5 %copy-start = (f32[1,4,32,16,128]{4,3,2,1,0:T(8,128)S(1)}, f32[1,4,32,16,128]{4,3,2,1,0:T(8,128)}, u32[]{:S(2)}) copy-start(f32[1,4,32,16,128]{4,3,2,1,0:T(8,128)} %param.12) | copy-start | bytes 3145732
  93.8 14.7 %copy-start.21 = (s32[1,16,128]{2,1,0:T(8,128)S(1)}, s32[1,16,128]{2,1,0:T(8,128)}, u32[]{:S(2)}) copy-start(s32[1,16,128]{2,1,0:T(8,128)} %param.14) | copy-start | bytes 24580
  97.4 112.3 %all-to-all-start.1 = ((f32[4,4,2048]{2,0,1:T(4,128)}), f32[4,4,2048]{2,0,1:T(4,128)S(1)}, u32[]{:S(2)}, u32[]{:S(2)}) async-start(f32[4,4,2048]{2,0,1:T(4,128)} %broadcast_multiply_fusion.1), calls=%async_computation.1 | async-start | bytes 262144 | tf_op jit(solution)/shard_map/all_to_all | solution.py:106
  103.0 79.6 %collective-permute-start = (f32[4,32,1,128]{3,2,1,0:T(1,128)}, f32[4,32,1,128]{3,2,1,0:T(1,128)}, u32[]{:S(2)}, u32[]{:S(2)}) collective-permute-start(f32[4,32,1,128]{3,2,1,0:T(1,128)} %get-tuple-element.55), channel_id=1, source_target_pairs={{0,32},{32,64},{64,96},{96,128},{128,160},{160,192},{192,224},{1,3... | collective-permute-start | bytes 196616 | tf_op jit(solution)/shard_map/ppermute | solution.py:25
  107.1 75.4 %collective-permute-start.1 = (f32[4,32,1,128]{3,2,1,0:T(1,128)}, f32[4,32,1,128]{3,2,1,0:T(1,128)}, u32[]{:S(2)}, u32[]{:S(2)}) collective-permute-start(f32[4,32,1,128]{3,2,1,0:T(1,128)} %get-tuple-element.56), channel_id=1, source_target_pairs={{32,0},{64,32},{96,64},{128,96},{160,128},{192,160},{224,192},{33,... | collective-permute-start | bytes 196616 | tf_op jit(solution)/shard_map/ppermute | solution.py:26
  108.5 1.5 copy-start.1
  110.0 0.8 copy-start.20
  188.4 12.5 %collective-permute-start.2 = (f32[4,32,18,1]{1,0,3,2:T(4,128)}, f32[4,32,18,1]{1,0,3,2:T(4,128)}, u32[]{:S(2)}, u32[]{:S(2)}) collective-permute-start(f32[4,32,18,1]{1,0,3,2:T(4,128)} %copy.54), channel_id=1, source_target_pairs={{0,4},{4,8},{8,12},{12,16},{16,20},{20,24},{24,28},{1,5},{5,9},{9,... | collective-permute-start | bytes 27656 | tf_op jit(solution)/shard_map/ppermute | solution.py:25
  192.8 10.6 %collective-permute-start.3 = (f32[4,32,18,1]{1,0,3,2:T(4,128)}, f32[4,32,18,1]{1,0,3,2:T(4,128)}, u32[]{:S(2)}, u32[]{:S(2)}) collective-permute-start(f32[4,32,18,1]{1,0,3,2:T(4,128)} %copy.56), channel_id=1, source_target_pairs={{4,0},{8,4},{12,8},{16,12},{20,16},{24,20},{28,24},{5,1},{9,5},{13... | collective-permute-start | bytes 27656 | tf_op jit(solution)/shard_map/ppermute | solution.py:26
  209.7 8.8 %all-to-all-start = ((f32[1,4,2048]{2,0,1:T(1,128)}), f32[1,4,2048]{2,0,1:T(1,128)S(1)}, u32[]{:S(2)}, u32[]{:S(2)}) async-start(f32[1,4,2048]{2,0,1:T(1,128)} %bitcast.17), calls=%async_computation | async-start | bytes 65536 | tf_op jit(solution)/shard_map/all_to_all | solution.py:113
  218.5 7.2 %copy-start.12 = (f32[1,4,2048]{2,0,1:T(1,128)}, f32[1,4,2048]{2,0,1:T(1,128)S(1)}, u32[]{:S(2)}) copy-start(f32[1,4,2048]{2,0,1:T(1,128)S(1)} %all-to-all-done) | copy-start | bytes 98308
  220.1 7.5 %all-to-all-start.2 = ((f32[4,1,2048]{2,1,0:T(1,128)}), f32[4,1,2048]{2,1,0:T(1,128)S(1)}, u32[]{:S(2)}, u32[]{:S(2)}) async-start(f32[4,1,2048]{2,1,0:T(1,128)} %copy.64), calls=%async_computation.2 | async-start | bytes 65536 | tf_op jit(solution)/shard_map/all_to_all | solution.py:118
  223.7 2.8 copy-start.14
  224.8 70.7 %copy-start.3 = (f32[8,8192]{1,0:T(8,128)}, f32[8,8192]{1,0:T(8,128)S(1)}, u32[]{:S(2)}) copy-start(f32[8,8192]{1,0:T(8,128)S(1)} %get-tuple-element.31) | copy-start | bytes 786436
  278.9 16.7 %copy-start.9 = (s32[8192]{0:T(1024)S(1)}, s32[8192]{0:T(1024)}, u32[]{:S(2)}) copy-start(s32[8192]{0:T(1024)} %copy-done.8) | copy-start | bytes 98308
  334.0 2.9 copy-start.11
  337.5 6.7 %collective-permute-start.4 = (f32[4,32,1,128]{3,2,1,0:T(1,128)S(1)}, f32[4,32,1,128]{3,2,1,0:T(1,128)S(1)}, u32[]{:S(2)}, u32[]{:S(2)}) collective-permute-start(f32[4,32,1,128]{3,2,1,0:T(1,128)S(1)} %get-tuple-element.48), channel_id=1, source_target_pairs={{0,32},{32,64},{64,96},{96,128},{128,160},{160,192},{192,224},{1,3... | collective-permute-start | bytes 196616 | tf_op jit(solution)/shard_map/ppermute | solution.py:25
  341.5 5.0 %collective-permute-start.5 = (f32[4,32,1,128]{3,2,1,0:T(1,128)S(1)}, f32[4,32,1,128]{3,2,1,0:T(1,128)S(1)}, u32[]{:S(2)}, u32[]{:S(2)}) collective-permute-start(f32[4,32,1,128]{3,2,1,0:T(1,128)S(1)} %get-tuple-element.49), channel_id=1, source_target_pairs={{32,0},{64,32},{96,64},{128,96},{160,128},{192,160},{224,192},{33,... | collective-permute-start | bytes 196616 | tf_op jit(solution)/shard_map/ppermute | solution.py:26
  344.2 2.2 copy-start.16
  346.5 0.6 copy-start.17
  351.5 14.4 %collective-permute-start.6 = (f32[4,32,18,1]{1,0,3,2:T(4,128)}, f32[4,32,18,1]{1,0,3,2:T(4,128)}, u32[]{:S(2)}, u32[]{:S(2)}) collective-permute-start(f32[4,32,18,1]{1,0,3,2:T(4,128)} %copy.67), channel_id=1, source_target_pairs={{0,4},{4,8},{8,12},{12,16},{16,20},{20,24},{24,28},{1,5},{5,9},{9,... | collective-permute-start | bytes 27656 | tf_op jit(solution)/shard_map/ppermute | solution.py:25
  359.2 8.1 %collective-permute-start.7 = (f32[4,32,18,1]{1,0,3,2:T(4,128)}, f32[4,32,18,1]{1,0,3,2:T(4,128)}, u32[]{:S(2)}, u32[]{:S(2)}) collective-permute-start(f32[4,32,18,1]{1,0,3,2:T(4,128)} %copy.69), channel_id=1, source_target_pairs={{4,0},{8,4},{12,8},{16,12},{20,16},{24,20},{28,24},{5,1},{9,5},{13... | collective-permute-start | bytes 27656 | tf_op jit(solution)/shard_map/ppermute | solution.py:26
  362.6 12.0 %all-to-all-start.3 = ((f32[4,4,2048]{2,0,1:T(4,128)}), f32[4,4,2048]{2,0,1:T(4,128)S(1)}, u32[]{:S(2)}, u32[]{:S(2)}) async-start(f32[4,4,2048]{2,0,1:T(4,128)} %broadcast_multiply_fusion), calls=%async_computation.3 | async-start | bytes 262144 | tf_op jit(solution)/shard_map/all_to_all | solution.py:106
  373.5 1.0 copy-start.2
  373.6 1.2 copy-start.13
  373.6 1.2 copy-start.18
  373.6 7.2 %copy-start.5 = (f32[1,1,1,7,8192]{4,3,2,1,0:T(8,128)S(1)}, f32[1,1,1,7,8192]{4,3,2,1,0:T(8,128)}, u32[]{:S(2)}) copy-start(f32[1,1,1,7,8192]{4,3,2,1,0:T(8,128)} %get-tuple-element.33) | copy-start | bytes 688132
  373.6 7.2 %copy-start.6 = (f32[1,1,1,7,8192]{4,3,2,1,0:T(8,128)S(1)}, f32[1,1,1,7,8192]{4,3,2,1,0:T(8,128)}, u32[]{:S(2)}) copy-start(f32[1,1,1,7,8192]{4,3,2,1,0:T(8,128)} %get-tuple-element.29) | copy-start | bytes 688132
  373.6 7.2 %copy-start.7 = (f32[7,8192]{1,0:T(8,128)S(1)}, f32[7,8192]{1,0:T(8,128)}, u32[]{:S(2)}) copy-start(f32[7,8192]{1,0:T(8,128)} %get-tuple-element.30) | copy-start | bytes 688132
  373.6 7.2 %copy-start.15 = (f32[1,8192]{1,0:T(1,128)S(1)}, f32[1,8192]{1,0:T(1,128)}, u32[]{:S(2)}) copy-start(f32[1,8192]{1,0:T(1,128)} %copy-done.14) | copy-start | bytes 98308
  373.6 7.2 %copy-start.19 = (f32[1,1,1,1,8192]{4,3,2,1,0:T(1,128)S(1)}, f32[1,1,1,1,8192]{4,3,2,1,0:T(1,128)}, u32[]{:S(2)}) copy-start(f32[1,1,1,1,8192]{4,3,2,1,0:T(1,128)} %subtract_multiply_fusion) | copy-start | bytes 98308
  375.5 8.5 %all-to-all-start.4 = ((f32[4,1,2048]{2,1,0:T(1,128)}), f32[4,1,2048]{2,1,0:T(1,128)S(1)}, u32[]{:S(2)}, u32[]{:S(2)}) async-start(f32[4,1,2048]{2,1,0:T(1,128)} %copy.78), calls=%async_computation.4 | async-start | bytes 65536 | tf_op jit(solution)/shard_map/all_to_all | solution.py:118
  436.1 1.0 copy-start.4
where the time goes:
time: 443 us; the launch traced here: 437 us
  local copies, waits for them, and re-layouts  208 us (47%)
  other arithmetic  127 us (29%)
  blocking collectives  47.9 us (11%)
  starting transfers between devices  44.2 us (10%)
  waiting for transfers between devices  9.33 us (2%)
    scatter-add x2, other arithmetic, local(): heat_term = jnp.zeros((cell_total,), jnp.float32).at[slot_cell].add(-WALL...  101 us
    gather x4, local copies, waits for them, and re-layouts, local(): send_buffer = flat_field[:, slot_cell] * valid_slots[None, :]  82.6 us
    all_gather x2, blocking collectives, local(): lax.all_gather(precursor[:, step_index:step_index + 1], 'inflow', axis=3,...  47.9 us
    gather x2, local copies, waits for them, and re-layouts, inlet_planes(): taken = jnp.take(window, relative, axis=2).astype(jnp.float32)  20.9 us
    unnamed x50, local copies, waits for them, and re-layouts  20.9 us
    scatter-add x1, local copies, waits for them, and re-layouts, update(): return updated.at[3].add(heat_term)  16.6 us
    ppermute x4, starting transfers between devices, extended(): before = lax.ppermute(last, axis, up)  16.5 us
    scatter x1, local copies, waits for them, and re-layouts, local(): valid_slots = jnp.zeros((columns,), jnp.float32).at[slot_index].set(1.0)  16.1 us
  transfers between devices with their start and end apart: 13, of which 4 were waited for; matrix products, arithmetic and copies ran while one was open for 15% of the time, Pallas kernels for 0%

commit v1 on v0

v1 whole, which is shorter than its diff:
```python
import functools

import jax
import jax.numpy as jnp
from jax import lax
from jax.experimental import pallas as pl
from jax.experimental.pallas import tpu as pltpu
from jax.sharding import PartitionSpec as P

F32, BF16, I32 = jnp.float32, jnp.bfloat16, jnp.int32
MESH = pl.DeviceIdType.MESH

XL, CY, CZ, NV = 32, 16, 128, 4
CAP, LAYERS, FACES = 2048, 8, 4096
N_FLUID, N_INFLOW, N_SOLID = 8, 8, 4
COLUMNS = N_SOLID * CAP
ROWS = FACES // 128

TIME_STEP = 0.1
VISCOSITY = 0.5
HEAT_TRANSFER = 0.8
CONDUCT_SLOPE = 0.2
SOLID_STEP = 0.15
WALL_WEIGHT = 0.5


def split(x):
    high = x.astype(BF16)
    return high, (x - high.astype(F32)).astype(BF16)


def transfer_of(u, v, w):
    return HEAT_TRANSFER * (1.0 + 0.5 * (u * u + v * v + w * w))


def iota(shape, dim):
    return lax.broadcasted_iota(I32, shape, dim)


def bits(mask):
    return jnp.where(mask, 1.0, 0.0).astype(BF16)


def dot(a, b):
    return lax.dot_general(a, b, (((1,), (0,)), ((), ())), preferred_element_type=F32)


def dot_t(a, b):
    return lax.dot_general(a, b, (((1,), (1,)), ((), ())), preferred_element_type=F32)


def kernel(
    state,
    prec,
    imap,
    fcell,
    fown,
    wall,
    out_state,
    out_wall,
    q0,
    q1,
    ob,
    wv,
    pv,
    imv,
    fcv,
    fov,
    psend,
    win,
    wsend,
    wrecv,
    hy_send,
    hy_recv,
    hz_send,
    hz_recv,
    fsend,
    frecv,
    oh_cell,
    oh_slot,
    oh_in,
    vm,
    lhs,
    wl,
    kcell,
    rcell,
    kslot,
    rslot,
    kin,
    rin,
    count,
    s_sum,
    i_sum,
    f_sum,
    a_face,
    b_face,
    t_face,
    i_face,
    f_face,
    load_sem,
    p_send_sem,
    p_recv_sem,
    w_send_sem,
    w_recv_sem,
    h_send_sem,
    h_recv_sem,
    f_send_sem,
    f_recv_sem,
    out_sem,
):
    fl, inf, so = lax.axis_index("fluid"), lax.axis_index("inflow"), lax.axis_index("solid")

    loads = [
        pltpu.make_async_copy(prec, pv, load_sem.at[0]),
        pltpu.make_async_copy(wall, wv, load_sem.at[1]),
        pltpu.make_async_copy(state, q0.at[:, pl.ds(1, XL)], load_sem.at[2]),
        pltpu.make_async_copy(fown, fov, load_sem.at[3]),
        pltpu.make_async_copy(fcell, fcv, load_sem.at[4]),
        pltpu.make_async_copy(imap, imv, load_sem.at[5]),
    ]
    for load in loads:
        load.start()

    barrier = pltpu.get_barrier_semaphore()

    def greet(ids):
        pl.semaphore_signal(barrier, inc=1, device_id=ids, device_id_type=MESH)

    for d in range(1, N_INFLOW):
        greet({"inflow": lax.rem(inf + d, N_INFLOW)})
    for d in (1, N_FLUID - 1):
        greet({"fluid": lax.rem(fl + d, N_FLUID)})
    for d in range(1, N_SOLID):
        greet({"solid": lax.rem(so + d, N_SOLID)})

    lane = iota((CY, CZ), 1)
    row = iota((CY, CZ), 0)

    loads[0].wait()
    for s in range(2):
        for k in range(16):
            psend[s, pl.ds(k, 4, stride=16), :] = pv[s, :, k * 128 : (k + 1) * 128].astype(F32)
    for s in range(2):
        win[s, inf] = psend[s].astype(BF16)
    loads[1].wait()
    for t in range(64):
        wsend[pl.ds(t // 16 * 32 + t % 16, 2, stride=16), :] = wv[0:2, t * 128 : (t + 1) * 128]
    loads[2].wait()

    def pack_edges(x, values, packed):
        low, high = packed
        for c in range(NV):
            k = c * XL + x
            low = jnp.where(lane == k, pltpu.roll(values[c], k, 1), low)
            high = jnp.where(lane == k, pltpu.roll(values[c], lax.rem(k + 1, 128), 1), high)
            hy = values[c]
            keep_row(c, x, hy)
        return low, high

    def keep_row(c, x, value):
        k = c * XL + x
        hy_now[0, pl.ds(k, 1), :] = value[0:1]
        hy_now[1, pl.ds(k, 1), :] = value[CY - 1 : CY]

    hy_now = hy_send.at[0]

    def edges_of(x, packed):
        return pack_edges(x, [q0[c, x + 1] for c in range(NV)], packed)

    zero_plane = jnp.zeros((CY, CZ), F32)
    low, high = lax.fori_loop(0, XL, edges_of, (zero_plane, zero_plane))
    hz_send[0, 0] = low
    hz_send[0, 1] = high
    for c in range(NV):
        q0[c, XL + 1] = q0[c, XL]

    pl.semaphore_wait(barrier, (N_INFLOW - 1) + 2 + (N_SOLID - 1))

    wall_copies = []
    for d in range(1, N_SOLID):
        to = lax.rem(so + d, N_SOLID)
        wall_copies.append(
            pltpu.make_async_remote_copy(
                src_ref=wsend.at[pl.ds(pl.multiple_of(to * 32, 32), 32)],
                dst_ref=wrecv.at[pl.ds(pl.multiple_of(so * 32, 32), 32)],
                send_sem=w_send_sem.at[d - 1],
                recv_sem=w_recv_sem.at[d - 1],
                device_id={"solid": to},
                device_id_type=MESH,
            )
        )

    def halo_copies(step):
        copies = []
        for side in range(2):
            far = N_FLUID - 1 if side == 0 else 1
            copies.append(
                pltpu.make_async_remote_copy(
                    src_ref=hy_send.at[step, side],
                    dst_ref=hy_recv.at[step, 1 - side],
                    send_sem=h_send_sem.at[step, 0, side],
                    recv_sem=h_recv_sem.at[step, 0, side],
                    device_id={"fluid": lax.rem(fl + far, N_FLUID)},
                    device_id_type=MESH,
                )
            )
        for side in range(2):
            far = N_INFLOW - 1 if side == 0 else 1
            copies.append(
                pltpu.make_async_remote_copy(
                    src_ref=hz_send.at[step, side],
                    dst_ref=hz_recv.at[step, 1 - side],
                    send_sem=h_send_sem.at[step, 1, side],
                    recv_sem=h_recv_sem.at[step, 1, side],
                    device_id={"inflow": lax.rem(inf + far, N_INFLOW)},
                    device_id_type=MESH,
                )
            )
        return copies

    def precursor_copies(step):
        return [
            pltpu.make_async_remote_copy(
                src_ref=win.at[step, inf],
                dst_ref=win.at[step, inf],
                send_sem=p_send_sem.at[step, d - 1],
                recv_sem=p_recv_sem.at[step, d - 1],
                device_id={"inflow": lax.rem(inf + d, N_INFLOW)},
                device_id_type=MESH,
            )
            for d in range(1, N_INFLOW)
        ]

    def precursor_arrivals(step):
        for d in range(1, N_INFLOW):
            came = lax.rem(inf + N_INFLOW - d, N_INFLOW)
            pltpu.make_async_remote_copy(
                src_ref=win.at[step, came],
                dst_ref=win.at[step, came],
                send_sem=p_send_sem.at[step, d - 1],
                recv_sem=p_recv_sem.at[step, d - 1],
                device_id={"inflow": came},
                device_id_type=MESH,
            ).wait_recv()

    def wall_arrivals():
        for d in range(1, N_SOLID):
            came = lax.rem(so + N_SOLID - d, N_SOLID)
            pltpu.make_async_remote_copy(
                src_ref=wsend.at[pl.ds(pl.multiple_of(came * 32, 32), 32)],
                dst_ref=wrecv.at[pl.ds(pl.multiple_of(came * 32, 32), 32)],
                send_sem=w_send_sem.at[d - 1],
                recv_sem=w_recv_sem.at[d - 1],
                device_id={"solid": came},
                device_id_type=MESH,
            ).wait_recv()

    def flux_copies(step):
        copies = []
        for d in range(1, N_SOLID):
            to = lax.rem(so + d, N_SOLID)
            copies.append(
                pltpu.make_async_remote_copy(
                    src_ref=fsend.at[step, pl.ds(pl.multiple_of(to * 16, 16), 16)],
                    dst_ref=frecv.at[step, pl.ds(pl.multiple_of(so * 16, 16), 16)],
                    send_sem=f_send_sem.at[step, d - 1],
                    recv_sem=f_recv_sem.at[step, d - 1],
                    device_id={"solid": to},
                    device_id_type=MESH,
                )
            )
        return copies

    def flux_arrivals(step):
        for d in range(1, N_SOLID):
            came = lax.rem(so + N_SOLID - d, N_SOLID)
            pltpu.make_async_remote_copy(
                src_ref=fsend.at[step, pl.ds(pl.multiple_of(came * 16, 16), 16)],
                dst_ref=frecv.at[step, pl.ds(pl.multiple_of(came * 16, 16), 16)],
                send_sem=f_send_sem.at[step, d - 1],
                recv_sem=f_recv_sem.at[step, d - 1],
                device_id={"solid": came},
                device_id_type=MESH,
            ).wait_recv()

    sent = wall_copies + halo_copies(0) + precursor_copies(0) + precursor_copies(1)
    halos_0 = sent[N_SOLID - 1 : N_SOLID + 3]
    for copy in sent:
        copy.start()

    for load in loads[3:]:
        load.wait()
    cell = fcv[...]
    kcell[...] = lax.shift_right_logical(cell, 14) * 128 + (cell & 127)
    rcell[...] = lax.shift_right_logical(cell, 7) & 127
    owner = fov[...]
    marks = jnp.concatenate([jnp.where(owner == o, 1.0, 0.0) for o in range(N_SOLID)], axis=0)
    upper = jnp.where(iota((128, 128), 0) < iota((128, 128), 1), 1.0, 0.0)
    earlier = dot(
        marks.astype(BF16), jnp.concatenate([upper, jnp.ones((128, 128), F32)], axis=1).astype(BF16)
    )
    r_out, r_in = iota((128, 128), 0), iota((128, 128), 1)
    same = lax.shift_right_logical(r_out, 5) == lax.shift_right_logical(r_in, 5)
    below = bits(jnp.logical_and(same, r_in < r_out))
    ranks = (earlier[:, :128] + dot(below, earlier[:, 128:].astype(BF16))) * marks
    rank = ranks[0:32] + ranks[32:64] + ranks[64:96] + ranks[96:128]
    slot = owner * CAP + rank.astype(I32)
    hi = lax.shift_right_logical(slot, 7)
    kslot[...] = lax.shift_right_logical(hi, 5) * 128 + (slot & 127)
    rslot[...] = hi & 31
    relative = imv[...] - fl * (N_INFLOW * CAP)
    hi = lax.shift_right_logical(relative, 7)
    kin[...] = lax.shift_right_logical(hi, 6) * 128 + (relative & 127)
    rin[...] = hi & 63

    for j in range(ROWS):
        oh_cell[:, j * 128 : (j + 1) * 128] = bits(iota((512, 128), 0) == kcell[j : j + 1, :])
    for j in range(ROWS):
        oh_slot[:, j * 128 : (j + 1) * 128] = bits(iota((256, 128), 0) == kslot[j : j + 1, :])
    for j in range(CY):
        oh_in[:, j * 128 : (j + 1) * 128] = bits(iota((256, 128), 0) == kin[j : j + 1, :])

    def scatter_cells(fields):
        for j in range(ROWS):
            mask = iota((128, 128), 0) == rcell[j : j + 1, :]
            for i, field in enumerate(fields):
                vm[i * 128 : (i + 1) * 128, j * 128 : (j + 1) * 128] = jnp.where(
                    mask, field[j : j + 1, :], 0.0
                ).astype(BF16)
        return dot_t(vm[0 : len(fields) * 128, :], oh_cell[...])

    def halves(x):
        high, low = split(x)
        return high.astype(F32), low.astype(F32)

    count[...] = scatter_cells([jnp.ones((ROWS, 128), F32)])

    def store_sample_plane(quarter, xr, u, v, w, temp):
        at = pl.multiple_of(xr * CY, CY)
        parts = split(transfer_of(u, v, w)) + split(temp)
        for i, part in enumerate(parts):
            lhs[pl.ds(i * 128 + at, CY), quarter * 128 : (quarter + 1) * 128] = part

    def sample_faces():
        def chunk(n, _):
            cols = oh_cell[:, pl.ds(pl.multiple_of(n * 512, 512), 512)]
            found = dot(lhs[...], cols)
            for j in range(4):
                at = n * 4 + j
                mask = iota((128, 128), 0) == rcell[pl.ds(at, 1), :]
                part = found[:, j * 128 : (j + 1) * 128]
                for ref, base in ((a_face, 0), (b_face, 256)):
                    both = part[base : base + 128] + part[base + 128 : base + 256]
                    ref[pl.ds(at, 1), :] = jnp.sum(jnp.where(mask, both, 0.0), axis=0, keepdims=True)
            return 0

        lax.fori_loop(0, FACES // 512, chunk, 0)

    for quarter in range(4):

        def plane(xr, _):
            x = quarter * 8 + xr
            store_sample_plane(quarter, xr, *[q0[c, x + 1] for c in range(NV)])
            return 0

        lax.fori_loop(0, 8, plane, 0)
    sample_faces()

    own = pl.multiple_of(so * 32, 32)
    wrecv[pl.ds(own, 32)] = wsend[pl.ds(own, 32)]
    wall_arrivals()
    for o in range(N_SOLID):
        for layer in range(2):
            for i, part in enumerate(split(wrecv[o * 32 + layer * 16 : o * 32 + layer * 16 + 16, :])):
                at = (layer * 2 + i) * 32 + (o & 1) * 16
                wl[at : at + 16, (o >> 1) * 128 : (o >> 1) * 128 + 128] = part

    def wall_chunk(n, _):
        cols = oh_slot[:, pl.ds(pl.multiple_of(n * 512, 512), 512)]
        found = dot(wl[...], cols)
        for j in range(4):
            at = n * 4 + j
            mask = iota((32, 128), 0) == rslot[pl.ds(at, 1), :]
            part = found[:, j * 128 : (j + 1) * 128]
            for ref, base in ((t_face, 0), (i_face, 64)):
                both = part[base : base + 32] + part[base + 32 : base + 64]
                ref[pl.ds(at, 1), :] = jnp.sum(jnp.where(mask, both, 0.0), axis=0, keepdims=True)
        return 0

    lax.fori_loop(0, FACES // 512, wall_chunk, 0)
    t0 = t_face[...]
    t1 = i_face[...]
    i_face[...] = (
        0.5 * (jnp.exp(CONDUCT_SLOPE * t0) + jnp.exp(CONDUCT_SLOPE * t1)) * (t1 - t0)
    )

    sums = scatter_cells(halves(t_face[...]))
    s_sum[...] = sums[0:128] + sums[128:256]

    def inlet(step, dst):
        for g in range(CY // 4):
            window = jnp.concatenate(
                [win[step, 0:4].reshape(256, 128), win[step, 4:8].reshape(256, 128)], axis=1
            )
            found = dot(window, oh_in[:, g * 512 : (g + 1) * 512])
            for j in range(4):
                y = g * 4 + j
                index = rin[y : y + 1, :]
                part = found[:, j * 128 : (j + 1) * 128]
                for c in range(NV):
                    total = None
                    for src in range(4):
                        mask = iota((16, 128), 0) + src * 16 == index
                        term = jnp.where(mask, part[src * 64 + c * 16 : src * 64 + c * 16 + 16], 0.0)
                        total = term if total is None else total + term
                    dst[c, 0, y : y + 1, :] = jnp.sum(total, axis=0, keepdims=True)

    precursor_arrivals(0)
    inlet(0, q0)

    def neighbours(src, hy, zlow, zhigh, x, c, q):
        k = c * XL + x
        y_low = jnp.where(fl > 0, hy[0, pl.ds(k, 1), :], 0.0)
        y_high = jnp.where(fl < N_FLUID - 1, hy[1, pl.ds(k, 1), :], 0.0)
        minus_y = jnp.where(row == 0, y_low, pltpu.roll(q, 1, 0))
        plus_y = jnp.where(row == CY - 1, y_high, pltpu.roll(q, CY - 1, 0))
        minus_z = jnp.where(
            lane == 0, pltpu.roll(zlow, lax.rem(128 - k, 128), 1), pltpu.roll(q, 1, 1)
        )
        plus_z = jnp.where(lane == CZ - 1, pltpu.roll(zhigh, 127 - k, 1), pltpu.roll(q, CZ - 1, 1))
        return src[c, x], src[c, x + 2], minus_y, plus_y, minus_z, plus_z

    def advanced(src, hy, zlow, zhigh, x):
        centre = [src[c, x + 1] for c in range(NV)]
        u, v, w, _ = centre
        fresh = []
        for c in range(NV):
            q = centre[c]
            xm, xp, ym, yp, zm, zp = neighbours(src, hy, zlow, zhigh, x, c, q)
            laplace = xm + xp + ym + yp + zm + zp - 6.0 * q
            advection = 0.5 * (u * (xp - xm) + v * (yp - ym) + w * (zp - zm))
            fresh.append(q + TIME_STEP * (VISCOSITY * laplace - advection))
        return centre, fresh

    for copy in halos_0:
        copy.wait_recv()
    zlow_0 = jnp.where(inf > 0, hz_recv[0, 0], 0.0)
    zhigh_0 = jnp.where(inf < N_INFLOW - 1, hz_recv[0, 1], 0.0)
    hy_now = hy_send.at[1]
    packed = (zero_plane, zero_plane)
    for quarter in range(4):

        def first(xr, packed):
            x = quarter * 8 + xr
            at = pl.multiple_of(xr * CY, CY)
            cols = slice(quarter * 128, (quarter + 1) * 128)
            centre, fresh = advanced(q0, hy_recv.at[0], zlow_0, zhigh_0, x)
            u, v, w, temp = centre
            total = transfer_of(u, v, w) * (
                count[pl.ds(at, CY), cols] * temp - s_sum[pl.ds(at, CY), cols]
            )
            f_sum[pl.ds(at, CY), cols] = total
            fresh[3] = fresh[3] - WALL_WEIGHT * total
            for c in range(NV):
                q1[c, x + 1] = fresh[c]
            store_sample_plane(quarter, xr, *fresh)
            return pack_edges(x, fresh, packed)

        packed = lax.fori_loop(0, 8, first, packed)
    hz_send[1, 0] = packed[0]
    hz_send[1, 1] = packed[1]
    halos_1 = halo_copies(1)
    for copy in halos_1:
        copy.start()
    for c in range(NV):
        q1[c, XL + 1] = q1[c, XL]

    def send_flux(step, flux):
        parts = halves(flux)
        for j in range(ROWS):
            mask = iota((32, 128), 0) == rslot[j : j + 1, :]
            for i, part in enumerate(parts):
                vm[i * 32 : (i + 1) * 32, j * 128 : (j + 1) * 128] = jnp.where(
                    mask, part[j : j + 1, :], 0.0
                ).astype(BF16)
        found = dot_t(vm[0:64, :], oh_slot[...])
        both = found[0:32] + found[32:64]
        for o in range(N_SOLID):
            fsend[step, o * 16 : (o + 1) * 16] = both[
                (o & 1) * 16 : (o & 1) * 16 + 16, (o >> 1) * 128 : (o >> 1) * 128 + 128
            ]
        copies = flux_copies(step)
        for copy in copies:
            copy.start()
        own = pl.multiple_of(so * 16, 16)
        frecv[step, pl.ds(own, 16)] = fsend[step, pl.ds(own, 16)]
        return copies

    flux = a_face[...] * (b_face[...] - t_face[...])
    f_face[...] = flux
    flux_0 = send_flux(0, flux)

    sample_faces()
    t_later = t_face[...] + SOLID_STEP * (i_face[...] + f_face[...])
    flux_1 = send_flux(1, a_face[...] * (b_face[...] - t_later))

    sums = scatter_cells(halves(i_face[...]))
    i_sum[...] = s_sum[...] + SOLID_STEP * (sums[0:128] + sums[128:256] + f_sum[...])

    precursor_arrivals(1)
    inlet(1, q1)
    for copy in halos_1:
        copy.wait_recv()
    zlow_1 = jnp.where(inf > 0, hz_recv[1, 0], 0.0)
    zhigh_1 = jnp.where(inf < N_INFLOW - 1, hz_recv[1, 1], 0.0)
    outs = []
    for quarter in range(4):

        def second(xr, _):
            x = quarter * 8 + xr
            at = pl.multiple_of(xr * CY, CY)
            cols = slice(quarter * 128, (quarter + 1) * 128)
            centre, fresh = advanced(q1, hy_recv.at[1], zlow_1, zhigh_1, x)
            u, v, w, temp = centre
            total = transfer_of(u, v, w) * (
                count[pl.ds(at, CY), cols] * temp - i_sum[pl.ds(at, CY), cols]
            )
            fresh[3] = fresh[3] - WALL_WEIGHT * total
            for c in range(NV):
                ob[c, x] = fresh[c]
            return 0

        lax.fori_loop(0, 8, second, 0)
        out = pltpu.make_async_copy(
            ob.at[:, pl.ds(quarter * 8, 8)],
            out_state.at[:, pl.ds(quarter * 8, 8)],
            out_sem.at[quarter],
        )
        out.start()
        outs.append(out)

    layer = iota((LAYERS, 128), 0)

    def conduct(temps, flux_row):
        conductivity = jnp.exp(CONDUCT_SLOPE * temps)
        above = pltpu.roll(temps, LAYERS - 1, 0)
        c_above = pltpu.roll(conductivity, LAYERS - 1, 0)
        flow = jnp.where(
            layer == LAYERS - 1,
            conductivity * (0.0 - temps),
            0.5 * (conductivity + c_above) * (above - temps),
        )
        from_below = jnp.where(layer == 0, flux_row, -pltpu.roll(flow, 1, 0))
        return temps + SOLID_STEP * (flow + from_below)

    flux_arrivals(0)
    flux_arrivals(1)

    def wall_tile(t, _):
        cols = pl.ds(pl.multiple_of(t * 128, 128), 128)
        temps = conduct(wv[:, cols], frecv[0, pl.ds(t, 1), :])
        wv[:, cols] = conduct(temps, frecv[1, pl.ds(t, 1), :])
        return 0

    lax.fori_loop(0, COLUMNS // 128, wall_tile, 0, unroll=4)
    out = pltpu.make_async_copy(wv, out_wall, out_sem.at[4])
    out.start()
    outs.append(out)
    for copy in sent + halos_1 + flux_0 + flux_1:
        copy.wait_send()
    for out in outs:
        out.wait()


def local(state, precursor, inlet_map, face_cell, face_owner, wall_temp):
    any_space = pl.BlockSpec(memory_space=pl.ANY)
    vmem = pltpu.VMEM
    dma = pltpu.SemaphoreType.DMA
    new_state, new_wall = pl.pallas_call(
        kernel,
        out_shape=(
            jax.ShapeDtypeStruct((NV, XL, CY, CZ), F32),
            jax.ShapeDtypeStruct((LAYERS, COLUMNS), F32),
        ),
        in_specs=[any_space] * 6,
        out_specs=(any_space, any_space),
        scratch_shapes=[
            vmem((NV, XL + 2, CY, CZ), F32),
            vmem((NV, XL + 2, CY, CZ), F32),
            vmem((NV, XL, CY, CZ), F32),
            vmem((LAYERS, COLUMNS), F32),
            vmem((2, NV, CAP), BF16),
            vmem((CY, CZ), I32),
            vmem((ROWS, 128), I32),
            vmem((ROWS, 128), I32),
            vmem((2, 64, 128), F32),
            vmem((2, N_INFLOW, 64, 128), BF16),
            vmem((128, 128), F32),
            vmem((128, 128), F32),
            vmem((2, 2, 128, 128), F32),
            vmem((2, 2, 128, 128), F32),
            vmem((2, 2, CY, 128), F32),
            vmem((2, 2, CY, 128), F32),
            vmem((2, 64, 128), F32),
            vmem((2, 64, 128), F32),
            vmem((512, FACES), BF16),
            vmem((256, FACES), BF16),
            vmem((256, CY * CZ), BF16),
            vmem((256, FACES), BF16),
            vmem((512, 512), BF16),
            vmem((128, 256), BF16),
            vmem((ROWS, 128), I32),
            vmem((ROWS, 128), I32),
            vmem((ROWS, 128), I32),
            vmem((ROWS, 128), I32),
            vmem((CY, 128), I32),
            vmem((CY, 128), I32),
            vmem((128, 512), F32),
            vmem((128, 512), F32),
            vmem((128, 512), F32),
            vmem((128, 512), F32),
            vmem((ROWS, 128), F32),
            vmem((ROWS, 128), F32),
            vmem((ROWS, 128), F32),
            vmem((ROWS, 128), F32),
            vmem((ROWS, 128), F32),
            dma((6,)),
            dma((2, N_INFLOW - 1)),
            dma((2, N_INFLOW - 1)),
            dma((N_SOLID - 1,)),
            dma((N_SOLID - 1,)),
            dma((2, 2, 2)),
            dma((2, 2, 2)),
            dma((2, N_SOLID - 1)),
            dma((2, N_SOLID - 1)),
            dma((5,)),
        ],
        compiler_params=pltpu.CompilerParams(
            collective_id=0, has_side_effects=True, vmem_limit_bytes=48 * 1024 * 1024
        ),
        name="manifold_step",
    )(
        state[0],
        precursor[0],
        inlet_map[0],
        face_cell.reshape(ROWS, 128),
        face_owner.reshape(ROWS, 128),
        wall_temp[0, 0, 0],
    )
    return new_state[None], new_wall[None, None, None]


def solution(mesh):
    return jax.shard_map(
        local,
        mesh=mesh,
        in_specs=(
            P("solid", None, None, "fluid", "inflow"),
            P("solid", None, None, ("fluid", "inflow")),
            P("solid", "fluid", "inflow"),
            P("solid", "fluid", "inflow", None),
            P("solid", "fluid", "inflow", None, None),
            P("solid", "fluid", "inflow", None, None),
        ),
        out_specs=(
            P("solid", None, None, "fluid", "inflow"),
            P("solid", "fluid", "inflow", None, None),
        ),
        check_vma=False,
    )
```

time: 443 us -> 46.8 us (0.11); the launches traced: 437 us -> 46.5 us
  local copies, waits for them, and re-layouts: 208 us -> 6.73 us
  other arithmetic: 127 us -> 0 us
  blocking collectives: 47.9 us -> 0 us
  starting transfers between devices: 44.2 us -> 0 us
  Pallas kernels: 0 us -> 39.1 us
  waiting for transfers between devices: 9.33 us -> 0 us
    gather x6 -> x0, local copies, waits for them, and re-layouts: 103 us -> none  [the longest x4 82.6 us: local(): send_buffer = flat_field[:, slot_cell] * valid_slots[None, :]]
    scatter-add x4 -> x0, other arithmetic: 102 us -> none  [the longest x2 101 us: local(): heat_term = jnp.zeros((cell_total,), jnp.float32).at[slot_cell].add(-WALL...]
    all_gather x2 -> x0, blocking collectives: 47.9 us -> none  [local(): lax.all_gather(precursor[:, step_index:step_index + 1], 'inflow', axis=3,...]
    pallas_call x0 -> x1, Pallas kernels: none -> 39.1 us  [local(): pl.pallas_call(kernel, out_shape=(jax.ShapeDtypeStruct((NV, XL, CY, CZ),...]
    scatter x2 -> x0, local copies, waits for them, and re-layouts: 31.8 us -> none  [the longest x1 16.1 us: local(): valid_slots = jnp.zeros((columns,), jnp.float32).at[slot_index].set(1.0)]
    ppermute x8 -> x0, starting transfers between devices: 23.9 us -> none  [the longest x4 16.5 us: extended(): before = lax.ppermute(last, axis, up)]
    all_to_all x5 -> x0, starting transfers between devices: 20.3 us -> none  [the longest x2 8.16 us: local(): lax.all_to_all(send_buffer.reshape(components, solid_count, CAP), 'solid'...]
    slice x17 -> x0, local copies, waits for them, and re-layouts: 18.5 us -> none  [the longest x6 9.7 us: extended(): last = lax.slice_in_dim(shard, length - width, length, axis=dim)]
  transfers between devices with their start and end apart: 13 -> 0, of which waited for: 4 -> 0; matrix products, arithmetic and copies ran while one was open for 15% -> 0% of each run, Pallas kernels for 0% -> 0%
where the time goes in v1:
time: 46.8 us; the launch traced here: 46.5 us
  Pallas kernels  39.1 us (84%)
  local copies, waits for them, and re-layouts  6.73 us (14%)
  between operations  0.65 us (1%)
    pallas_call x1, Pallas kernels, local(): pl.pallas_call(kernel, out_shape=(jax.ShapeDtypeStruct((NV, XL, CY, CZ),...  39.1 us
    unnamed x14, local copies, waits for them, and re-layouts  6.73 us

profile of v1, /device:TPU:1, one launch (start us, length us, event | category | flops | bytes accessed | tf_op | source)
XLA Modules:
  0.0 46.5 jit_solution(5245789306214216876)
XLA Ops:
  0.6 0.0 copy-start.5
  0.6 0.7 %copy-done.5 = s32[1,16,128]{2,1,0:T(8,128)S(1)} copy-done((s32[1,16,128]{2,1,0:T(8,128)S(1)}, s32[1,16,128]{2,1,0:T(8,128)}, u32[]{:S(2)}) %copy-start.5) | copy-done | bytes 8216
  1.3 0.0 copy-start
  1.3 1.2 %copy-done = f32[1,4,32,16,128]{4,3,2,1,0:T(8,128)S(1)} copy-done((f32[1,4,32,16,128]{4,3,2,1,0:T(8,128)S(1)}, f32[1,4,32,16,128]{4,3,2,1,0:T(8,128)}, u32[]{:S(2)}) %copy-start) | copy-done | bytes 1048600
  2.6 0.0 copy-start.1
  2.6 0.9 %copy-done.1 = f32[1,1,1,8,8192]{4,3,2,1,0:T(8,128)S(1)} copy-done((f32[1,1,1,8,8192]{4,3,2,1,0:T(8,128)S(1)}, f32[1,1,1,8,8192]{4,3,2,1,0:T(8,128)}, u32[]{:S(2)}) %copy-start.1) | copy-done | bytes 262168
  3.5 0.0 copy-start.2
  3.5 0.8 %copy-done.2 = bf16[1,2,4,2048]{3,2,1,0:T(4,128)(2,1)S(1)} copy-done((bf16[1,2,4,2048]{3,2,1,0:T(4,128)(2,1)S(1)}, bf16[1,2,4,2048]{3,2,1,0:T(4,128)(2,1)}, u32[]{:S(2)}) %copy-start.2) | copy-done | bytes 32792
  4.3 0.0 copy-start.3
  4.3 0.7 %copy-done.3 = s32[1,1,1,4096]{3,2,1,0:T(1,128)S(1)} copy-done((s32[1,1,1,4096]{3,2,1,0:T(1,128)S(1)}, s32[1,1,1,4096]{3,2,1,0:T(1,128)}, u32[]{:S(2)}) %copy-start.3) | copy-done | bytes 16408
  5.0 0.0 copy-start.4
  5.0 0.7 %copy-done.4 = s32[1,1,1,4096,1]{3,4,2,1,0:T(1,128)S(1)} copy-done((s32[1,1,1,4096,1]{3,4,2,1,0:T(1,128)S(1)}, s32[1,1,1,4096,1]{3,4,2,1,0:T(1,128)}, u32[]{:S(2)}) %copy-start.4) | copy-done | bytes 16408
  5.7 39.1 %manifold_step.1 = (f32[4,32,16,128]{3,2,1,0:T(8,128)S(1)}, f32[8,8192]{1,0:T(8,128)S(1)}) custom-call(f32[4,32,16,128]{3,2,1,0:T(8,128)S(1)} %bitcast.8, bf16[2,4,2048]{2,1,0:T(4,128)(2,1)S(1)} %bitcast.12, s32[16,128]{1,0:T(8,128)S(1)} %bitcast.15, s32[32,128]{1,0:T(8,128)S(1)} %bitcast.13, s32[32,128]{1,0:T(8,128)S(1)} %bitcast.14, f32[8,8192]{1,0:T(8,128)S(1)} %bitcast.11), custom_call_target="tpu_custom_call" | custom-call | tf_op jit(solution)/shard_map/manifold_step/pallas_call | solution.py:579
  44.8 1.0 %copy.10 = f32[1,4,32,16,128]{4,3,2,1,0:T(8,128)} copy(f32[1,4,32,16,128]{4,3,2,1,0:T(8,128)S(1)} %bitcast.9) | data formatting | bytes 2097152
  45.8 0.7 %copy.11 = f32[1,1,1,8,8192]{4,3,2,1,0:T(8,128)} copy(f32[1,1,1,8,8192]{4,3,2,1,0:T(8,128)S(1)} %bitcast.10) | data formatting | bytes 524288
Async XLA Ops:
  0.6 0.7 %copy-start.5 = (s32[1,16,128]{2,1,0:T(8,128)S(1)}, s32[1,16,128]{2,1,0:T(8,128)}, u32[]{:S(2)}) copy-start(s32[1,16,128]{2,1,0:T(8,128)} %param.8) | copy-start | bytes 24580
  1.3 1.2 %copy-start = (f32[1,4,32,16,128]{4,3,2,1,0:T(8,128)S(1)}, f32[1,4,32,16,128]{4,3,2,1,0:T(8,128)}, u32[]{:S(2)}) copy-start(f32[1,4,32,16,128]{4,3,2,1,0:T(8,128)} %param.6) | copy-start | bytes 3145732
  2.6 0.9 %copy-start.1 = (f32[1,1,1,8,8192]{4,3,2,1,0:T(8,128)S(1)}, f32[1,1,1,8,8192]{4,3,2,1,0:T(8,128)}, u32[]{:S(2)}) copy-start(f32[1,1,1,8,8192]{4,3,2,1,0:T(8,128)} %param.11) | copy-start | bytes 786436
  3.5 0.8 %copy-start.2 = (bf16[1,2,4,2048]{3,2,1,0:T(4,128)(2,1)S(1)}, bf16[1,2,4,2048]{3,2,1,0:T(4,128)(2,1)}, u32[]{:S(2)}) copy-start(bf16[1,2,4,2048]{3,2,1,0:T(4,128)(2,1)} %param.7) | copy-start | bytes 98308
  4.3 0.7 %copy-start.3 = (s32[1,1,1,4096]{3,2,1,0:T(1,128)S(1)}, s32[1,1,1,4096]{3,2,1,0:T(1,128)}, u32[]{:S(2)}) copy-start(s32[1,1,1,4096]{3,2,1,0:T(1,128)} %param.9) | copy-start | bytes 49156
  5.0 0.7 %copy-start.4 = (s32[1,1,1,4096,1]{3,4,2,1,0:T(1,128)S(1)}, s32[1,1,1,4096,1]{3,4,2,1,0:T(1,128)}, u32[]{:S(2)}) copy-start(s32[1,1,1,4096,1]{3,4,2,1,0:T(1,128)} %param.10) | copy-start | bytes 49156

commit v2 on v1

v2 whole, which is shorter than its diff:
```python
import functools

import jax
import jax.numpy as jnp
from jax import lax
from jax.experimental import pallas as pl
from jax.experimental.pallas import tpu as pltpu
from jax.sharding import PartitionSpec as P

F32, BF16, I32 = jnp.float32, jnp.bfloat16, jnp.int32
MESH = pl.DeviceIdType.MESH

XL, CY, CZ, NV = 32, 16, 128, 4
CAP, LAYERS, FACES = 2048, 8, 4096
N_FLUID, N_INFLOW, N_SOLID = 8, 8, 4
COLUMNS = N_SOLID * CAP
ROWS = FACES // 128
TOP, PITCH = 8, 32

TIME_STEP = 0.1
VISCOSITY = 0.5
HEAT_TRANSFER = 0.8
CONDUCT_SLOPE = 0.2
SOLID_STEP = 0.15
WALL_WEIGHT = 0.5


def split(x):
    high = x.astype(BF16)
    return high, (x - high.astype(F32)).astype(BF16)


def transfer_of(u, v, w):
    return HEAT_TRANSFER * (1.0 + 0.5 * (u * u + v * v + w * w))


def iota(shape, dim):
    return lax.broadcasted_iota(I32, shape, dim)


def bits(mask):
    return jnp.where(mask, 1.0, 0.0).astype(BF16)


def dot(a, b):
    return lax.dot_general(a, b, (((1,), (0,)), ((), ())), preferred_element_type=F32)


def dot_t(a, b):
    return lax.dot_general(a, b, (((1,), (1,)), ((), ())), preferred_element_type=F32)


def kernel(
    state,
    prec,
    imap,
    fcell,
    fown,
    wall,
    out_state,
    out_wall,
    q0,
    q1,
    ob,
    wv,
    pv,
    imv,
    fcv,
    fov,
    psend,
    win,
    wsend,
    wrecv,
    hy_send,
    hy_recv,
    hz_send,
    hz_recv,
    fsend,
    frecv,
    oh_cell,
    oh_slot,
    oh_in,
    oh_srow,
    vm,
    lhs,
    wl,
    zf,
    qf,
    rf,
    lf,
    hf,
    sf,
    zi,
    hi_in,
    ri,
    rcell,
    rslot,
    count,
    s_sum,
    i_sum,
    a_face,
    b_face,
    t_face,
    i_face,
    load_sem,
    p_send_sem,
    p_recv_sem,
    w_send_sem,
    w_recv_sem,
    h_send_sem,
    h_recv_sem,
    f_send_sem,
    f_recv_sem,
    out_sem,
):
    fl, inf, so = lax.axis_index("fluid"), lax.axis_index("inflow"), lax.axis_index("solid")

    loads = [
        pltpu.make_async_copy(prec, pv, load_sem.at[0]),
        pltpu.make_async_copy(wall, wv, load_sem.at[1]),
        pltpu.make_async_copy(state, q0.at[:, pl.ds(1, XL), pl.ds(TOP, CY)], load_sem.at[2]),
        pltpu.make_async_copy(fown, fov, load_sem.at[3]),
        pltpu.make_async_copy(fcell, fcv, load_sem.at[4]),
        pltpu.make_async_copy(imap, imv, load_sem.at[5]),
    ]
    for load in loads:
        load.start()

    barrier = pltpu.get_barrier_semaphore()

    def greet(ids):
        pl.semaphore_signal(barrier, inc=1, device_id=ids, device_id_type=MESH)

    for d in range(1, N_INFLOW):
        greet({"inflow": lax.rem(inf + d, N_INFLOW)})
    for d in (1, N_FLUID - 1):
        greet({"fluid": lax.rem(fl + d, N_FLUID)})
    for d in range(1, N_SOLID):
        greet({"solid": lax.rem(so + d, N_SOLID)})

    lane = iota((CY, CZ), 1)

    loads[0].wait()
    for s in range(2):
        for k in range(16):
            psend[s, pl.ds(k, 4, stride=16), :] = pv[s, :, k * 128 : (k + 1) * 128].astype(F32)
    for s in range(2):
        win[s, inf] = psend[s].astype(BF16)
    loads[1].wait()
    for t in range(64):
        wsend[pl.ds(t // 16 * 32 + t % 16, 2, stride=16), :] = wv[0:2, t * 128 : (t + 1) * 128]

    wall_copies = []
    for d in range(1, N_SOLID):
        to = lax.rem(so + d, N_SOLID)
        wall_copies.append(
            pltpu.make_async_remote_copy(
                src_ref=wsend.at[pl.ds(pl.multiple_of(to * 32, 32), 32)],
                dst_ref=wrecv.at[pl.ds(pl.multiple_of(so * 32, 32), 32)],
                send_sem=w_send_sem.at[d - 1],
                recv_sem=w_recv_sem.at[d - 1],
                device_id={"solid": to},
                device_id_type=MESH,
            )
        )

    def halo_copies(step):
        copies = []
        for side in range(2):
            far = N_FLUID - 1 if side == 0 else 1
            copies.append(
                pltpu.make_async_remote_copy(
                    src_ref=hy_send.at[step, side],
                    dst_ref=hy_recv.at[step, 1 - side],
                    send_sem=h_send_sem.at[step, 0, side],
                    recv_sem=h_recv_sem.at[step, 0, side],
                    device_id={"fluid": lax.rem(fl + far, N_FLUID)},
                    device_id_type=MESH,
                )
            )
        for side in range(2):
            far = N_INFLOW - 1 if side == 0 else 1
            copies.append(
                pltpu.make_async_remote_copy(
                    src_ref=hz_send.at[step],
                    dst_ref=hz_recv.at[step, 1 - side],
                    send_sem=h_send_sem.at[step, 1, side],
                    recv_sem=h_recv_sem.at[step, 1, side],
                    device_id={"inflow": lax.rem(inf + far, N_INFLOW)},
                    device_id_type=MESH,
                )
            )
        return copies

    precursor_copies = [
        pltpu.make_async_remote_copy(
            src_ref=win.at[:, inf],
            dst_ref=win.at[:, inf],
            send_sem=p_send_sem.at[d - 1],
            recv_sem=p_recv_sem.at[d - 1],
            device_id={"inflow": lax.rem(inf + d, N_INFLOW)},
            device_id_type=MESH,
        )
        for d in range(1, N_INFLOW)
    ]

    def precursor_arrivals():
        for d in range(1, N_INFLOW):
            came = lax.rem(inf + N_INFLOW - d, N_INFLOW)
            pltpu.make_async_remote_copy(
                src_ref=win.at[:, came],
                dst_ref=win.at[:, came],
                send_sem=p_send_sem.at[d - 1],
                recv_sem=p_recv_sem.at[d - 1],
                device_id={"inflow": came},
                device_id_type=MESH,
            ).wait_recv()

    def wall_arrivals():
        for d in range(1, N_SOLID):
            came = lax.rem(so + N_SOLID - d, N_SOLID)
            pltpu.make_async_remote_copy(
                src_ref=wsend.at[pl.ds(pl.multiple_of(came * 32, 32), 32)],
                dst_ref=wrecv.at[pl.ds(pl.multiple_of(came * 32, 32), 32)],
                send_sem=w_send_sem.at[d - 1],
                recv_sem=w_recv_sem.at[d - 1],
                device_id={"solid": came},
                device_id_type=MESH,
            ).wait_recv()

    flux_copies = []
    for d in range(1, N_SOLID):
        to = lax.rem(so + d, N_SOLID)
        flux_copies.append(
            pltpu.make_async_remote_copy(
                src_ref=fsend.at[:, pl.ds(pl.multiple_of(to * 16, 16), 16)],
                dst_ref=frecv.at[:, pl.ds(pl.multiple_of(so * 16, 16), 16)],
                send_sem=f_send_sem.at[d - 1],
                recv_sem=f_recv_sem.at[d - 1],
                device_id={"solid": to},
                device_id_type=MESH,
            )
        )

    def flux_arrivals():
        for d in range(1, N_SOLID):
            came = lax.rem(so + N_SOLID - d, N_SOLID)
            pltpu.make_async_remote_copy(
                src_ref=fsend.at[:, pl.ds(pl.multiple_of(came * 16, 16), 16)],
                dst_ref=frecv.at[:, pl.ds(pl.multiple_of(came * 16, 16), 16)],
                send_sem=f_send_sem.at[d - 1],
                recv_sem=f_recv_sem.at[d - 1],
                device_id={"solid": came},
                device_id_type=MESH,
            ).wait_recv()

    pl.semaphore_wait(barrier, (N_INFLOW - 1) + 2 + (N_SOLID - 1))
    for copy in wall_copies + precursor_copies:
        copy.start()

    def pair_of(c, x):
        return (c % 2) * XL + x

    def keep_edges(step, x, values, packed):
        packed = list(packed)
        for c in range(NV):
            k = c * XL + x
            hy_send[step, 0, pl.ds(k, 1), :] = values[c][0:1]
            hy_send[step, 1, pl.ds(k, 1), :] = values[c][CY - 1 : CY]
            j = pair_of(c, x)
            moved = pltpu.roll(values[c], 2 * j + 1, 1)
            packed[c // 2] = jnp.where(lax.shift_right_logical(lane, 1) == j, moved, packed[c // 2])
        return tuple(packed)

    zero_plane = jnp.zeros((CY, CZ), F32)
    loads[2].wait()

    def edges_of(x, packed):
        values = [q0[c, x + 1, TOP : TOP + CY, :] for c in range(NV)]
        keep_sample_plane(x, *values)
        return keep_edges(0, x, values, packed)

    def keep_sample_plane(x, u, v, w, temp):
        parts = split(transfer_of(u, v, w)) + split(temp)
        quarter = lax.shift_right_logical(x, 3)
        at = pl.multiple_of((x & 7) * CY, CY)
        for i, part in enumerate(parts):
            lhs[quarter, pl.ds(i * 128 + at, CY), :] = part

    packed = lax.fori_loop(0, XL, edges_of, (zero_plane, zero_plane), unroll=4)
    hz_send[0, 0] = packed[0]
    hz_send[0, 1] = packed[1]
    halos_0 = halo_copies(0)
    for copy in halos_0:
        copy.start()
    for c in range(NV):
        q0[c, XL + 1, TOP : TOP + CY, :] = q0[c, XL, TOP : TOP + CY, :]

    for load in loads[3:]:
        load.wait()
    cell = fcv[...]
    qf[...] = lax.shift_right_logical(cell, 14).astype(F32)
    zf[...] = (cell & 127).astype(F32)
    r = lax.shift_right_logical(cell, 7) & 127
    rcell[...] = r
    rf[...] = r.astype(F32)
    owner = fov[...]
    marks = jnp.concatenate([jnp.where(owner == o, 1.0, 0.0) for o in range(N_SOLID)], axis=0)
    upper = jnp.where(iota((128, 128), 0) < iota((128, 128), 1), 1.0, 0.0)
    earlier = dot(
        marks.astype(BF16), jnp.concatenate([upper, jnp.ones((128, 128), F32)], axis=1).astype(BF16)
    )
    r_out, r_in = iota((128, 128), 0), iota((128, 128), 1)
    same = lax.shift_right_logical(r_out, 5) == lax.shift_right_logical(r_in, 5)
    below = bits(jnp.logical_and(same, r_in < r_out))
    ranks = (earlier[:, :128] + dot(below, earlier[:, 128:].astype(BF16))) * marks
    rank = ranks[0:32] + ranks[32:64] + ranks[64:96] + ranks[96:128]
    slot = owner * CAP + rank.astype(I32)
    hi = lax.shift_right_logical(slot, 7)
    hf[...] = lax.shift_right_logical(hi, 5).astype(F32)
    lf[...] = (slot & 127).astype(F32)
    rslot[...] = hi & 31
    sf[...] = (hi & 31).astype(F32)
    relative = imv[...] - fl * (N_INFLOW * CAP)
    hi = lax.shift_right_logical(relative, 7)
    zi[...] = (relative & 127).astype(F32)
    hi_in[...] = lax.shift_right_logical(hi, 6).astype(F32)
    ri[...] = hi & 63

    steps_128 = iota((128, 128), 0).astype(F32).astype(BF16)
    one, zero = jnp.ones((), BF16), jnp.zeros((), BF16)

    def wide(row_values, blocks):
        tile = jnp.broadcast_to(row_values, (16, 128)).astype(BF16)
        return jnp.concatenate([tile] * blocks, axis=0) if blocks > 1 else tile

    def hot(row_values, blocks):
        return jnp.where(steps_128[: blocks * 16] == wide(row_values, blocks), one, zero)

    def marked(row_values, value, blocks):
        return wide(jnp.where(row_values == value, 1.0, 0.0), blocks)

    for j in range(ROWS):
        cols = slice(j * 128, (j + 1) * 128)
        base = hot(zf[j : j + 1, :], 8)
        for part in range(4):
            oh_cell[part * 128 : (part + 1) * 128, cols] = base * marked(
                qf[j : j + 1, :], float(part), 8
            )
        vm[0:128, cols] = hot(rf[j : j + 1, :], 8)
    for j in range(ROWS):
        cols = slice(j * 128, (j + 1) * 128)
        base = hot(lf[j : j + 1, :], 8)
        for part in range(2):
            oh_slot[part * 128 : (part + 1) * 128, cols] = base * marked(
                hf[j : j + 1, :], float(part), 8
            )
        oh_srow[:, cols] = hot(sf[j : j + 1, :], 2)
    for j in range(CY):
        cols = slice(j * 128, (j + 1) * 128)
        base = hot(zi[j : j + 1, :], 8)
        for part in range(2):
            oh_in[part * 128 : (part + 1) * 128, cols] = base * marked(
                hi_in[j : j + 1, :], float(part), 8
            )

    def sample_faces():
        fields = jnp.concatenate([lhs[i] for i in range(4)], axis=1)

        def chunk(n, _):
            cols = oh_cell[:, pl.ds(pl.multiple_of(n * 512, 512), 512)]
            found = dot(fields, cols)
            for j in range(4):
                at = n * 4 + j
                mask = iota((128, 128), 0) == rcell[pl.ds(at, 1), :]
                part = found[:, j * 128 : (j + 1) * 128]
                for ref, base in ((a_face, 0), (b_face, 256)):
                    both = part[base : base + 128] + part[base + 128 : base + 256]
                    ref[pl.ds(at, 1), :] = jnp.sum(jnp.where(mask, both, 0.0), axis=0, keepdims=True)
            return 0

        lax.fori_loop(0, FACES // 512, chunk, 0, unroll=2)

    sample_faces()

    own = pl.multiple_of(so * 32, 32)
    wrecv[pl.ds(own, 32)] = wsend[pl.ds(own, 32)]
    wall_arrivals()
    for o in range(N_SOLID):
        for layer in range(2):
            for i, part in enumerate(split(wrecv[o * 32 + layer * 16 : o * 32 + layer * 16 + 16, :])):
                at = (layer * 2 + i) * 32 + (o & 1) * 16
                wl[at : at + 16, (o >> 1) * 128 : (o >> 1) * 128 + 128] = part

    def wall_chunk(n, _):
        cols = oh_slot[:, pl.ds(pl.multiple_of(n * 512, 512), 512)]
        found = dot(wl[...], cols)
        for j in range(4):
            at = n * 4 + j
            mask = iota((32, 128), 0) == rslot[pl.ds(at, 1), :]
            part = found[:, j * 128 : (j + 1) * 128]
            for ref, base in ((t_face, 0), (i_face, 64)):
                both = part[base : base + 32] + part[base + 32 : base + 64]
                ref[pl.ds(at, 1), :] = jnp.sum(jnp.where(mask, both, 0.0), axis=0, keepdims=True)
        return 0

    lax.fori_loop(0, FACES // 512, wall_chunk, 0, unroll=4)
    t0 = t_face[...]
    t1 = i_face[...]
    between = 0.5 * (jnp.exp(CONDUCT_SLOPE * t0) + jnp.exp(CONDUCT_SLOPE * t1)) * (t1 - t0)
    i_face[...] = between

    def halves(x):
        high, low = split(x)
        return high.astype(F32), low.astype(F32)

    fields = halves(t0) + halves(between)
    for j in range(ROWS):
        cols = slice(j * 128, (j + 1) * 128)
        marks = vm[0:128, cols]
        for i, field in enumerate(fields):
            vm[(i + 1) * 128 : (i + 2) * 128, cols] = marks * wide(field[j : j + 1, :], 8)
    sums = dot_t(vm[...], oh_cell[...])
    for part in range(4):
        cols, rows = slice(part * 128, (part + 1) * 128), slice(part * 128, (part + 1) * 128)
        count[rows, :] = sums[0:128, cols]
        s_sum[rows, :] = sums[128:256, cols] + sums[256:384, cols]
        i_sum[rows, :] = sums[384:512, cols] + sums[512:640, cols]

    precursor_arrivals()
    window = jnp.concatenate(
        [
            jnp.concatenate(
                [win[step, 0:4].reshape(256, 128), win[step, 4:8].reshape(256, 128)], axis=1
            )
            for step in range(2)
        ],
        axis=0,
    )
    for g in range(CY // 4):
        found = dot(window, oh_in[:, g * 512 : (g + 1) * 512])
        for j in range(4):
            y = g * 4 + j
            mask = iota((64, 128), 0) == ri[y : y + 1, :]
            for step, dst in ((0, q0), (1, q1)):
                part = found[step * 256 : (step + 1) * 256, j * 128 : (j + 1) * 128]
                for c in range(NV):
                    total = None
                    for src in range(4):
                        term = jnp.where(
                            mask[src * 16 : src * 16 + 16],
                            part[src * 64 + c * 16 : src * 64 + c * 16 + 16],
                            0.0,
                        )
                        total = term if total is None else total + term
                    dst[c, 0, TOP + y : TOP + y + 1, :] = jnp.sum(total, axis=0, keepdims=True)

    def receive_halos(step, copies, dst):
        for copy in copies:
            copy.wait_recv()

        def rows_of(x, _):
            for c in range(NV):
                k = c * XL + x
                dst[c, x + 1, TOP - 1 : TOP, :] = jnp.where(
                    fl > 0, hy_recv[step, 0, pl.ds(k, 1), :], 0.0
                )
                dst[c, x + 1, TOP + CY : TOP + CY + 1, :] = jnp.where(
                    fl < N_FLUID - 1, hy_recv[step, 1, pl.ds(k, 1), :], 0.0
                )
            return 0

        lax.fori_loop(0, XL, rows_of, 0, unroll=8)
        merged = []
        for part in range(2):
            low = jnp.where(inf > 0, pltpu.roll(hz_recv[step, 0, part], 1, 1), 0.0)
            high = jnp.where(inf < N_INFLOW - 1, pltpu.roll(hz_recv[step, 1, part], 127, 1), 0.0)
            merged.append(jnp.where((lane & 1) == 1, low, high))
        return merged

    first_lane, last_lane = lane == 0, lane == CZ - 1

    def advanced(src, merged, x):
        centre = [src[c, x + 1, TOP : TOP + CY, :] for c in range(NV)]
        half = 0.5 * TIME_STEP
        slopes = [half * speed for speed in centre[:3]]
        ahead = [VISCOSITY * TIME_STEP - slope for slope in slopes]
        behind = [VISCOSITY * TIME_STEP + slope for slope in slopes]
        fresh = []
        for c in range(NV):
            q = centre[c]
            j = pair_of(c, x)
            edge = pltpu.roll(merged[c // 2], 127 - 2 * j, 1)
            zm = jnp.where(first_lane, edge, pltpu.roll(q, 1, 1))
            zp = jnp.where(last_lane, edge, pltpu.roll(q, CZ - 1, 1))
            xm = src[c, x, TOP : TOP + CY, :]
            xp = src[c, x + 2, TOP : TOP + CY, :]
            ym = src[c, x + 1, TOP - 1 : TOP + CY - 1, :]
            yp = src[c, x + 1, TOP + 1 : TOP + CY + 1, :]
            along_x = ahead[0] * xp + behind[0] * xm
            along_y = ahead[1] * yp + behind[1] * ym
            along_z = ahead[2] * zp + behind[2] * zm
            fresh.append(
                (1.0 - 6.0 * VISCOSITY * TIME_STEP) * q + ((along_x + along_y) + along_z)
            )
        return centre, fresh

    merged_0 = receive_halos(0, halos_0, q0)

    def first(x, packed):
        rows = pl.ds(pl.multiple_of(x * CY, CY), CY)
        centre, fresh = advanced(q0, merged_0, x)
        u, v, w, temp = centre
        colder = s_sum[rows, :]
        total = transfer_of(u, v, w) * (count[rows, :] * temp - colder)
        i_sum[rows, :] = colder + SOLID_STEP * (i_sum[rows, :] + total)
        fresh[3] = fresh[3] - WALL_WEIGHT * total
        for c in range(NV):
            q1[c, x + 1, TOP : TOP + CY, :] = fresh[c]
        keep_sample_plane(x, *fresh)
        return keep_edges(1, x, fresh, packed)

    flux_0 = a_face[...] * (b_face[...] - t_face[...])
    packed = lax.fori_loop(0, XL, first, (zero_plane, zero_plane), unroll=2)
    hz_send[1, 0] = packed[0]
    hz_send[1, 1] = packed[1]
    halos_1 = halo_copies(1)
    for copy in halos_1:
        copy.start()
    for c in range(NV):
        q1[c, XL + 1, TOP : TOP + CY, :] = q1[c, XL, TOP : TOP + CY, :]

    sample_faces()
    t_later = t_face[...] + SOLID_STEP * (i_face[...] + flux_0)
    flux_1 = a_face[...] * (b_face[...] - t_later)
    parts = halves(flux_0) + halves(flux_1)
    for j in range(ROWS):
        cols = slice(j * 128, (j + 1) * 128)
        marks = oh_srow[:, cols]
        for i, part in enumerate(parts):
            vm[i * 32 : (i + 1) * 32, cols] = marks * wide(part[j : j + 1, :], 2)
    found = dot_t(vm[0:128, :], oh_slot[...])
    for step in range(2):
        both = found[step * 64 : step * 64 + 32] + found[step * 64 + 32 : step * 64 + 64]
        for o in range(N_SOLID):
            fsend[step, o * 16 : (o + 1) * 16] = both[
                (o & 1) * 16 : (o & 1) * 16 + 16, (o >> 1) * 128 : (o >> 1) * 128 + 128
            ]
    for copy in flux_copies:
        copy.start()
    own = pl.multiple_of(so * 16, 16)
    for step in range(2):
        frecv[step, pl.ds(own, 16)] = fsend[step, pl.ds(own, 16)]

    merged_1 = receive_halos(1, halos_1, q1)
    outs = []

    def second(x, _):
        rows = pl.ds(pl.multiple_of(x * CY, CY), CY)
        centre, fresh = advanced(q1, merged_1, x)
        u, v, w, temp = centre
        total = transfer_of(u, v, w) * (count[rows, :] * temp - i_sum[rows, :])
        fresh[3] = fresh[3] - WALL_WEIGHT * total
        for c in range(NV):
            ob[c, x] = fresh[c]
        return 0

    def second_half(part):
        lax.fori_loop(part * 16, part * 16 + 16, second, 0, unroll=2)
        out = pltpu.make_async_copy(
            ob.at[:, pl.ds(part * 16, 16)],
            out_state.at[:, pl.ds(part * 16, 16)],
            out_sem.at[part],
        )
        out.start()
        outs.append(out)

    second_half(0)

    layer = iota((LAYERS, 128), 0)

    def conduct(temps, flux_row):
        conductivity = jnp.exp(CONDUCT_SLOPE * temps)
        above = pltpu.roll(temps, LAYERS - 1, 0)
        c_above = pltpu.roll(conductivity, LAYERS - 1, 0)
        flow = jnp.where(
            layer == LAYERS - 1,
            conductivity * (0.0 - temps),
            0.5 * (conductivity + c_above) * (above - temps),
        )
        from_below = jnp.where(layer == 0, flux_row, -pltpu.roll(flow, 1, 0))
        return temps + SOLID_STEP * (flow + from_below)

    flux_arrivals()

    def wall_tiles(t, _):
        cols = [pl.ds(pl.multiple_of((t * 8 + i) * 128, 128), 128) for i in range(8)]
        temps = [wv[:, col] for col in cols]
        for step in range(2):
            rows = [frecv[step, pl.ds(t * 8 + i, 1), :] for i in range(8)]
            temps = [conduct(temp, flux_row) for temp, flux_row in zip(temps, rows)]
        for col, temp in zip(cols, temps):
            wv[:, col] = temp
        return 0

    lax.fori_loop(0, COLUMNS // 1024, wall_tiles, 0)
    out = pltpu.make_async_copy(wv, out_wall, out_sem.at[2])
    out.start()
    outs.append(out)

    second_half(1)
    for copy in wall_copies + precursor_copies + halos_0 + halos_1 + flux_copies:
        copy.wait_send()
    for out in outs:
        out.wait()


def local(state, precursor, inlet_map, face_cell, face_owner, wall_temp):
    any_space = pl.BlockSpec(memory_space=pl.ANY)
    vmem = pltpu.VMEM
    dma = pltpu.SemaphoreType.DMA
    new_state, new_wall = pl.pallas_call(
        kernel,
        out_shape=(
            jax.ShapeDtypeStruct((NV, XL, CY, CZ), F32),
            jax.ShapeDtypeStruct((LAYERS, COLUMNS), F32),
        ),
        in_specs=[any_space] * 6,
        out_specs=(any_space, any_space),
        scratch_shapes=[
            vmem((NV, XL + 2, PITCH, CZ), F32),
            vmem((NV, XL + 2, PITCH, CZ), F32),
            vmem((NV, XL, CY, CZ), F32),
            vmem((LAYERS, COLUMNS), F32),
            vmem((2, NV, CAP), BF16),
            vmem((CY, CZ), I32),
            vmem((ROWS, 128), I32),
            vmem((ROWS, 128), I32),
            vmem((2, 64, 128), F32),
            vmem((2, N_INFLOW, 64, 128), BF16),
            vmem((128, 128), F32),
            vmem((128, 128), F32),
            vmem((2, 2, 128, 128), F32),
            vmem((2, 2, 128, 128), F32),
            vmem((2, 2, CY, 128), F32),
            vmem((2, 2, 2, CY, 128), F32),
            vmem((2, 64, 128), F32),
            vmem((2, 64, 128), F32),
            vmem((512, FACES), BF16),
            vmem((256, FACES), BF16),
            vmem((256, CY * CZ), BF16),
            vmem((32, FACES), BF16),
            vmem((640, FACES), BF16),
            vmem((4, 512, 128), BF16),
            vmem((128, 256), BF16),
            vmem((ROWS, 128), F32),
            vmem((ROWS, 128), F32),
            vmem((ROWS, 128), F32),
            vmem((ROWS, 128), F32),
            vmem((ROWS, 128), F32),
            vmem((ROWS, 128), F32),
            vmem((CY, 128), F32),
            vmem((CY, 128), F32),
            vmem((CY, 128), I32),
            vmem((ROWS, 128), I32),
            vmem((ROWS, 128), I32),
            vmem((512, 128), F32),
            vmem((512, 128), F32),
            vmem((512, 128), F32),
            vmem((ROWS, 128), F32),
            vmem((ROWS, 128), F32),
            vmem((ROWS, 128), F32),
            vmem((ROWS, 128), F32),
            dma((6,)),
            dma((N_INFLOW - 1,)),
            dma((N_INFLOW - 1,)),
            dma((N_SOLID - 1,)),
            dma((N_SOLID - 1,)),
            dma((2, 2, 2)),
            dma((2, 2, 2)),
            dma((N_SOLID - 1,)),
            dma((N_SOLID - 1,)),
            dma((3,)),
        ],
        compiler_params=pltpu.CompilerParams(
            collective_id=0, has_side_effects=True, vmem_limit_bytes=62 * 1024 * 1024
        ),
        name="manifold_step",
    )(
        state[0],
        precursor[0],
        inlet_map[0],
        face_cell.reshape(ROWS, 128),
        face_owner.reshape(ROWS, 128),
        wall_temp[0, 0, 0],
    )
    return new_state[None], new_wall[None, None, None]


def solution(mesh):
    return jax.shard_map(
        local,
        mesh=mesh,
        in_specs=(
            P("solid", None, None, "fluid", "inflow"),
            P("solid", None, None, ("fluid", "inflow")),
            P("solid", "fluid", "inflow"),
            P("solid", "fluid", "inflow", None),
            P("solid", "fluid", "inflow", None, None),
            P("solid", "fluid", "inflow", None, None),
        ),
        out_specs=(
            P("solid", None, None, "fluid", "inflow"),
            P("solid", "fluid", "inflow", None, None),
        ),
        check_vma=False,
    )
```

time: 46.8 us -> 35.4 us (0.76)
  Pallas kernels: 39.1 us -> 31.3 us
  local copies, waits for them, and re-layouts: 6.73 us -> 3.03 us
    pallas_call x1, Pallas kernels: 39.1 us -> 31.3 us  [local(): pl.pallas_call(kernel, out_shape=(jax.ShapeDtypeStruct((NV, XL, CY, CZ),...]
    unnamed x14 -> x4, local copies, waits for them, and re-layouts: 6.73 us -> 3.03 us
where the time goes in v2:
time: 35.4 us; the launch traced here: 35 us
  Pallas kernels  31.3 us (88%)
  local copies, waits for them, and re-layouts  3.03 us (9%)
  between operations  0.65 us (2%)
    pallas_call x1, Pallas kernels, local(): pl.pallas_call(kernel, out_shape=(jax.ShapeDtypeStruct((NV, XL, CY, CZ),...  31.3 us
    unnamed x4, local copies, waits for them, and re-layouts  3.03 us

profile of v2, /device:TPU:1, one launch (start us, length us, event | category | flops | bytes accessed | tf_op | source)
XLA Modules:
  0.0 35.0 jit_solution(7552891948609648159)
XLA Ops:
  0.6 31.3 %manifold_step.1 = (f32[4,32,16,128]{3,2,1,0:T(8,128)}, f32[8,8192]{1,0:T(8,128)}) custom-call(f32[4,32,16,128]{3,2,1,0:T(8,128)} %bitcast.8, bf16[2,4,2048]{2,1,0:T(4,128)(2,1)} %bitcast.12, s32[16,128]{1,0:T(8,128)} %bitcast.15, s32[32,128]{1,0:T(8,128)} %bitcast.13, s32[32,128]{1,0:T(8,128)} %bitcast.14, f32[8,8192]{1,0:T(8,128)} %bitcast.11), custom_call_target="tpu_custom_call" | custom-call | tf_op jit(solution)/shard_map/manifold_step/pallas_call | solution.py:622
  31.9 0.0 copy-start
  31.9 2.3 %copy.10 = f32[1,4,32,16,128]{4,3,2,1,0:T(8,128)} copy(f32[1,4,32,16,128]{4,3,2,1,0:T(8,128)} %bitcast.9) | data formatting | bytes 2097152
  34.3 0.0 copy-done
  34.3 0.7 %copy.11 = f32[1,1,1,8,8192]{4,3,2,1,0:T(8,128)} copy(f32[1,1,1,8,8192]{4,3,2,1,0:T(8,128)S(1)} %bitcast.10) | data formatting | bytes 524288
Async XLA Ops:
  31.9 2.3 %copy-start = (f32[8,8192]{1,0:T(8,128)S(1)}, f32[8,8192]{1,0:T(8,128)}, u32[]{:S(2)}) copy-start(f32[8,8192]{1,0:T(8,128)} %get-tuple-element.5) | copy-start | bytes 786436

commit v3 on v2

--- a/solution.py
+++ b/solution.py
@@ -16,6 +16,9 @@
 COLUMNS = N_SOLID * CAP
 ROWS = FACES // 128
 TOP, PITCH = 8, 32
+CHUNK = 512
+CHUNKS = FACES // CHUNK
+PLANES = XL // CHUNKS
 
 TIME_STEP = 0.1
 VISCOSITY = 0.5
@@ -58,10 +61,9 @@
     fown,
     wall,
     out_state,
-    out_wall,
+    out_flux,
     q0,
     q1,
-    ob,
     wv,
     pv,
     imv,
@@ -82,7 +84,9 @@
     oh_in,
     oh_srow,
     vm,
-    lhs,
+    fm,
+    lhs_0,
+    lhs_1,
     wl,
     zf,
     qf,
@@ -97,11 +101,15 @@
     rslot,
     count,
     s_sum,
-    i_sum,
+    f_sum,
+    later,
     a_face,
     b_face,
     t_face,
     i_face,
+    f_face,
+    found_0,
+    found_1,
     load_sem,
     p_send_sem,
     p_recv_sem,
@@ -111,17 +119,16 @@
     h_recv_sem,
     f_send_sem,
     f_recv_sem,
-    out_sem,
 ):
     fl, inf, so = lax.axis_index("fluid"), lax.axis_index("inflow"), lax.axis_index("solid")
 
     loads = [
         pltpu.make_async_copy(prec, pv, load_sem.at[0]),
         pltpu.make_async_copy(wall, wv, load_sem.at[1]),
-        pltpu.make_async_copy(state, q0.at[:, pl.ds(1, XL), pl.ds(TOP, CY)], load_sem.at[2]),
         pltpu.make_async_copy(fown, fov, load_sem.at[3]),
         pltpu.make_async_copy(fcell, fcv, load_sem.at[4]),
         pltpu.make_async_copy(imap, imv, load_sem.at[5]),
+        pltpu.make_async_copy(state, q0.at[:, pl.ds(1, XL), pl.ds(TOP, CY)], load_sem.at[2]),
     ]
     for load in loads:
         load.start()
@@ -132,11 +139,11 @@
         pl.semaphore_signal(barrier, inc=1, device_id=ids, device_id_type=MESH)
 
     for d in range(1, N_INFLOW):
-        greet({"inflow": lax.rem(inf + d, N_INFLOW)})
+        greet({"inflow": (inf + d) & (N_INFLOW - 1)})
     for d in (1, N_FLUID - 1):
-        greet({"fluid": lax.rem(fl + d, N_FLUID)})
+        greet({"fluid": (fl + d) & (N_FLUID - 1)})
     for d in range(1, N_SOLID):
-        greet({"solid": lax.rem(so + d, N_SOLID)})
+        greet({"solid": (so + d) & (N_SOLID - 1)})
 
     lane = iota((CY, CZ), 1)
 
@@ -152,7 +159,7 @@
 
     wall_copies = []
     for d in range(1, N_SOLID):
-        to = lax.rem(so + d, N_SOLID)
+        to = (so + d) & (N_SOLID - 1)
         wall_copies.append(
             pltpu.make_async_remote_copy(
                 src_ref=wsend.at[pl.ds(pl.multiple_of(to * 32, 32), 32)],
@@ -174,7 +181,7 @@
                     dst_ref=hy_recv.at[step, 1 - side],
                     send_sem=h_send_sem.at[step, 0, side],
                     recv_sem=h_recv_sem.at[step, 0, side],
-                    device_id={"fluid": lax.rem(fl + far, N_FLUID)},
+                    device_id={"fluid": (fl + far) & (N_FLUID - 1)},
                     device_id_type=MESH,
                 )
             )
@@ -186,7 +193,7 @@
                     dst_ref=hz_recv.at[step, 1 - side],
                     send_sem=h_send_sem.at[step, 1, side],
                     recv_sem=h_recv_sem.at[step, 1, side],
-                    device_id={"inflow": lax.rem(inf + far, N_INFLOW)},
+                    device_id={"inflow": (inf + far) & (N_INFLOW - 1)},
                     device_id_type=MESH,
                 )
             )
@@ -198,7 +205,7 @@
             dst_ref=win.at[:, inf],
             send_sem=p_send_sem.at[d - 1],
             recv_sem=p_recv_sem.at[d - 1],
-            device_id={"inflow": lax.rem(inf + d, N_INFLOW)},
+            device_id={"inflow": (inf + d) & (N_INFLOW - 1)},
             device_id_type=MESH,
         )
         for d in range(1, N_INFLOW)
@@ -206,7 +213,7 @@
 
     def precursor_arrivals():
         for d in range(1, N_INFLOW):
-            came = lax.rem(inf + N_INFLOW - d, N_INFLOW)
+            came = (inf + N_INFLOW - d) & (N_INFLOW - 1)
             pltpu.make_async_remote_copy(
                 src_ref=win.at[:, came],
                 dst_ref=win.at[:, came],
@@ -218,7 +225,7 @@
 
     def wall_arrivals():
         for d in range(1, N_SOLID):
-            came = lax.rem(so + N_SOLID - d, N_SOLID)
+            came = (so + N_SOLID - d) & (N_SOLID - 1)
             pltpu.make_async_remote_copy(
                 src_ref=wsend.at[pl.ds(pl.multiple_of(came * 32, 32), 32)],
                 dst_ref=wrecv.at[pl.ds(pl.multiple_of(came * 32, 32), 32)],
@@ -228,23 +235,9 @@
                 device_id_type=MESH,
             ).wait_recv()
 
-    flux_copies = []
-    for d in range(1, N_SOLID):
-        to = lax.rem(so + d, N_SOLID)
-        flux_copies.append(
-            pltpu.make_async_remote_copy(
-                src_ref=fsend.at[:, pl.ds(pl.multiple_of(to * 16, 16), 16)],
-                dst_ref=frecv.at[:, pl.ds(pl.multiple_of(so * 16, 16), 16)],
-                send_sem=f_send_sem.at[d - 1],
-                recv_sem=f_recv_sem.at[d - 1],
-                device_id={"solid": to},
-                device_id_type=MESH,
-            )
-        )
-
     def flux_arrivals():
         for d in range(1, N_SOLID):
-            came = lax.rem(so + N_SOLID - d, N_SOLID)
+            came = (so + N_SOLID - d) & (N_SOLID - 1)
             pltpu.make_async_remote_copy(
                 src_ref=fsend.at[:, pl.ds(pl.multiple_of(came * 16, 16), 16)],
                 dst_ref=frecv.at[:, pl.ds(pl.multiple_of(came * 16, 16), 16)],
@@ -273,30 +266,17 @@
         return tuple(packed)
 
     zero_plane = jnp.zeros((CY, CZ), F32)
-    loads[2].wait()
-
-    def edges_of(x, packed):
-        values = [q0[c, x + 1, TOP : TOP + CY, :] for c in range(NV)]
-        keep_sample_plane(x, *values)
-        return keep_edges(0, x, values, packed)
-
-    def keep_sample_plane(x, u, v, w, temp):
-        parts = split(transfer_of(u, v, w)) + split(temp)
+    lhs = (lhs_0, lhs_1)
+
+    def keep_sample_plane(step, x, u, v, w, temp):
+        (a_high, a_low), (b_high, b_low) = split(transfer_of(u, v, w)), split(temp)
+        parts = (a_high, b_high, a_low, b_low)
         quarter = lax.shift_right_logical(x, 3)
         at = pl.multiple_of((x & 7) * CY, CY)
         for i, part in enumerate(parts):
-            lhs[quarter, pl.ds(i * 128 + at, CY), :] = part
-
-    packed = lax.fori_loop(0, XL, edges_of, (zero_plane, zero_plane), unroll=4)
-    hz_send[0, 0] = packed[0]
-    hz_send[0, 1] = packed[1]
-    halos_0 = halo_copies(0)
-    for copy in halos_0:
-        copy.start()
-    for c in range(NV):
-        q0[c, XL + 1, TOP : TOP + CY, :] = q0[c, XL, TOP : TOP + CY, :]
-
-    for load in loads[3:]:
+            lhs[step][quarter, pl.ds(i * 128 + at, CY), :] = part
+
+    for load in loads[2:5]:
         load.wait()
     cell = fcv[...]
     qf[...] = lax.shift_right_logical(cell, 14).astype(F32)
@@ -340,48 +320,76 @@
     def marked(row_values, value, blocks):
         return wide(jnp.where(row_values == value, 1.0, 0.0), blocks)
 
-    for j in range(ROWS):
-        cols = slice(j * 128, (j + 1) * 128)
-        base = hot(zf[j : j + 1, :], 8)
+    def lanes_of(j):
+        return pl.ds(pl.multiple_of(j * 128, 128), 128)
+
+    def one_hots_of_faces(j):
+        at, cols = pl.ds(j, 1), lanes_of(j)
+        base, quarter = hot(zf[at, :], 8), qf[at, :]
         for part in range(4):
-            oh_cell[part * 128 : (part + 1) * 128, cols] = base * marked(
-                qf[j : j + 1, :], float(part), 8
-            )
-        vm[0:128, cols] = hot(rf[j : j + 1, :], 8)
-    for j in range(ROWS):
-        cols = slice(j * 128, (j + 1) * 128)
-        base = hot(lf[j : j + 1, :], 8)
+            oh_cell[part * 128 : (part + 1) * 128, cols] = base * marked(quarter, float(part), 8)
+        vm[0:128, cols] = hot(rf[at, :], 8)
+        base, half = hot(lf[at, :], 8), hf[at, :]
         for part in range(2):
-            oh_slot[part * 128 : (part + 1) * 128, cols] = base * marked(
-                hf[j : j + 1, :], float(part), 8
-            )
-        oh_srow[:, cols] = hot(sf[j : j + 1, :], 2)
-    for j in range(CY):
-        cols = slice(j * 128, (j + 1) * 128)
-        base = hot(zi[j : j + 1, :], 8)
+            oh_slot[part * 128 : (part + 1) * 128, cols] = base * marked(half, float(part), 8)
+        oh_srow[:, cols] = hot(sf[at, :], 2)
+
+    def one_hots_of_inlet(j):
+        at, cols = pl.ds(j, 1), lanes_of(j)
+        base, half = hot(zi[at, :], 8), hi_in[at, :]
         for part in range(2):
-            oh_in[part * 128 : (part + 1) * 128, cols] = base * marked(
-                hi_in[j : j + 1, :], float(part), 8
-            )
-
-    def sample_faces():
-        fields = jnp.concatenate([lhs[i] for i in range(4)], axis=1)
-
-        def chunk(n, _):
-            cols = oh_cell[:, pl.ds(pl.multiple_of(n * 512, 512), 512)]
-            found = dot(fields, cols)
-            for j in range(4):
-                at = n * 4 + j
-                mask = iota((128, 128), 0) == rcell[pl.ds(at, 1), :]
-                part = found[:, j * 128 : (j + 1) * 128]
-                for ref, base in ((a_face, 0), (b_face, 256)):
-                    both = part[base : base + 128] + part[base + 128 : base + 256]
-                    ref[pl.ds(at, 1), :] = jnp.sum(jnp.where(mask, both, 0.0), axis=0, keepdims=True)
-            return 0
-
-        lax.fori_loop(0, FACES // 512, chunk, 0, unroll=2)
-
-    sample_faces()
+            oh_in[part * 128 : (part + 1) * 128, cols] = base * marked(half, float(part), 8)
+
+    loads[5].wait()
+
+    def prepare(n, packed):
+        for i in range(4):
+            x = n * 4 + i
+            values = [q0[c, x + 1, TOP : TOP + CY, :] for c in range(NV)]
+            keep_sample_plane(0, x, *values)
+            packed = keep_edges(0, x, values, packed)
+            one_hots_of_faces(n * 4 + i)
+        for i in range(2):
+            one_hots_of_inlet(n * 2 + i)
+        return packed
+
+    packed = lax.fori_loop(0, XL // 4, prepare, (zero_plane, zero_plane))
+    hz_send[0, 0] = packed[0]
+    hz_send[0, 1] = packed[1]
+    halos_0 = halo_copies(0)
+    for copy in halos_0:
+        copy.start()
+    for c in range(NV):
+        q0[c, XL + 1, TOP : TOP + CY, :] = q0[c, XL, TOP : TOP + CY, :]
+
+    def sample_product(step, n, found):
+        cols = oh_cell[:, pl.ds(pl.multiple_of(n * CHUNK, CHUNK), CHUNK)]
+        fields = jnp.concatenate([lhs[step][i] for i in range(4)], axis=1)
+        both = dot(fields, cols)
+        found[...] = both[0:256] + both[256:512]
+
+    def sample_pick(n, found):
+        for j in range(CHUNK // 128):
+            at = n * (CHUNK // 128) + j
+            cols = slice(j * 128, (j + 1) * 128)
+            mask = iota((128, 128), 0) == rcell[pl.ds(at, 1), :]
+            for ref, base in ((a_face, 0), (b_face, 128)):
+                both = found[base : base + 128, cols]
+                ref[pl.ds(at, 1), :] = jnp.sum(jnp.where(mask, both, 0.0), axis=0, keepdims=True)
+
+    def sample_faces(step, beside, carry):
+        sample_product(step, 0, found_0)
+
+        def two(m, carry):
+            sample_product(step, 2 * m + 1, found_1)
+            carry = beside(2 * m, carry)
+            sample_pick(2 * m, found_0)
+            sample_product(step, (2 * m + 2) & (CHUNKS - 1), found_0)
+            carry = beside(2 * m + 1, carry)
+            sample_pick(2 * m + 1, found_1)
+            return carry
+
+        return lax.fori_loop(0, CHUNKS // 2, two, carry)
 
     own = pl.multiple_of(so * 32, 32)
     wrecv[pl.ds(own, 32)] = wsend[pl.ds(own, 32)]
@@ -392,19 +400,15 @@
                 at = (layer * 2 + i) * 32 + (o & 1) * 16
                 wl[at : at + 16, (o >> 1) * 128 : (o >> 1) * 128 + 128] = part
 
-    def wall_chunk(n, _):
-        cols = oh_slot[:, pl.ds(pl.multiple_of(n * 512, 512), 512)]
-        found = dot(wl[...], cols)
+    for n in range(FACES // 512):
+        found = dot(wl[...], oh_slot[:, n * 512 : (n + 1) * 512])
         for j in range(4):
             at = n * 4 + j
-            mask = iota((32, 128), 0) == rslot[pl.ds(at, 1), :]
+            mask = iota((32, 128), 0) == rslot[at : at + 1, :]
             part = found[:, j * 128 : (j + 1) * 128]
             for ref, base in ((t_face, 0), (i_face, 64)):
                 both = part[base : base + 32] + part[base + 32 : base + 64]
-                ref[pl.ds(at, 1), :] = jnp.sum(jnp.where(mask, both, 0.0), axis=0, keepdims=True)
-        return 0
-
-    lax.fori_loop(0, FACES // 512, wall_chunk, 0, unroll=4)
+                ref[at : at + 1, :] = jnp.sum(jnp.where(mask, both, 0.0), axis=0, keepdims=True)
     t0 = t_face[...]
     t1 = i_face[...]
     between = 0.5 * (jnp.exp(CONDUCT_SLOPE * t0) + jnp.exp(CONDUCT_SLOPE * t1)) * (t1 - t0)
@@ -425,7 +429,7 @@
         cols, rows = slice(part * 128, (part + 1) * 128), slice(part * 128, (part + 1) * 128)
         count[rows, :] = sums[0:128, cols]
         s_sum[rows, :] = sums[128:256, cols] + sums[256:384, cols]
-        i_sum[rows, :] = sums[384:512, cols] + sums[512:640, cols]
+        f_sum[rows, :] = sums[384:512, cols] + sums[512:640, cols]
 
     precursor_arrivals()
     window = jnp.concatenate(
@@ -507,21 +511,23 @@
 
     merged_0 = receive_halos(0, halos_0, q0)
 
-    def first(x, packed):
-        rows = pl.ds(pl.multiple_of(x * CY, CY), CY)
-        centre, fresh = advanced(q0, merged_0, x)
-        u, v, w, temp = centre
-        colder = s_sum[rows, :]
-        total = transfer_of(u, v, w) * (count[rows, :] * temp - colder)
-        i_sum[rows, :] = colder + SOLID_STEP * (i_sum[rows, :] + total)
-        fresh[3] = fresh[3] - WALL_WEIGHT * total
-        for c in range(NV):
-            q1[c, x + 1, TOP : TOP + CY, :] = fresh[c]
-        keep_sample_plane(x, *fresh)
-        return keep_edges(1, x, fresh, packed)
-
-    flux_0 = a_face[...] * (b_face[...] - t_face[...])
-    packed = lax.fori_loop(0, XL, first, (zero_plane, zero_plane), unroll=2)
+    def first(n, packed):
+        for i in range(PLANES):
+            x = n * PLANES + i
+            rows = pl.ds(pl.multiple_of(x * CY, CY), CY)
+            centre, fresh = advanced(q0, merged_0, x)
+            u, v, w, temp = centre
+            colder = s_sum[rows, :]
+            total = transfer_of(u, v, w) * (count[rows, :] * temp - colder)
+            later[rows, :] = colder + SOLID_STEP * (f_sum[rows, :] + total)
+            fresh[3] = fresh[3] - WALL_WEIGHT * total
+            for c in range(NV):
+                q1[c, x + 1, TOP : TOP + CY, :] = fresh[c]
+            keep_sample_plane(1, x, *fresh)
+            packed = keep_edges(1, x, fresh, packed)
+        return packed
+
+    packed = sample_faces(0, first, (zero_plane, zero_plane))
     hz_send[1, 0] = packed[0]
     hz_send[1, 1] = packed[1]
     halos_1 = halo_copies(1)
@@ -530,22 +536,36 @@
     for c in range(NV):
         q1[c, XL + 1, TOP : TOP + CY, :] = q1[c, XL, TOP : TOP + CY, :]
 
-    sample_faces()
-    t_later = t_face[...] + SOLID_STEP * (i_face[...] + flux_0)
-    flux_1 = a_face[...] * (b_face[...] - t_later)
-    parts = halves(flux_0) + halves(flux_1)
+    flux_0 = a_face[...] * (b_face[...] - t_face[...])
+    t_face[...] = t_face[...] + SOLID_STEP * (i_face[...] + flux_0)
+    f_face[...] = flux_0
+    sample_faces(1, lambda n, carry: carry, 0)
+    parts = halves(f_face[...]) + halves(a_face[...] * (b_face[...] - t_face[...]))
     for j in range(ROWS):
         cols = slice(j * 128, (j + 1) * 128)
         marks = oh_srow[:, cols]
         for i, part in enumerate(parts):
-            vm[i * 32 : (i + 1) * 32, cols] = marks * wide(part[j : j + 1, :], 2)
-    found = dot_t(vm[0:128, :], oh_slot[...])
+            fm[i * 32 : (i + 1) * 32, cols] = marks * wide(part[j : j + 1, :], 2)
+    found = jnp.transpose(dot_t(oh_slot[...], fm[...]))
     for step in range(2):
         both = found[step * 64 : step * 64 + 32] + found[step * 64 + 32 : step * 64 + 64]
         for o in range(N_SOLID):
             fsend[step, o * 16 : (o + 1) * 16] = both[
                 (o & 1) * 16 : (o & 1) * 16 + 16, (o >> 1) * 128 : (o >> 1) * 128 + 128
             ]
+    flux_copies = []
+    for d in range(1, N_SOLID):
+        to = (so + d) & (N_SOLID - 1)
+        flux_copies.append(
+            pltpu.make_async_remote_copy(
+                src_ref=fsend.at[:, pl.ds(pl.multiple_of(to * 16, 16), 16)],
+                dst_ref=frecv.at[:, pl.ds(pl.multiple_of(so * 16, 16), 16)],
+                send_sem=f_send_sem.at[d - 1],
+                recv_sem=f_recv_sem.at[d - 1],
+                device_id={"solid": to},
+                device_id_type=MESH,
+            )
+        )
     for copy in flux_copies:
         copy.start()
     own = pl.multiple_of(so * 16, 16)
@@ -553,30 +573,34 @@
         frecv[step, pl.ds(own, 16)] = fsend[step, pl.ds(own, 16)]
 
     merged_1 = receive_halos(1, halos_1, q1)
-    outs = []
 
     def second(x, _):
         rows = pl.ds(pl.multiple_of(x * CY, CY), CY)
         centre, fresh = advanced(q1, merged_1, x)
         u, v, w, temp = centre
-        total = transfer_of(u, v, w) * (count[rows, :] * temp - i_sum[rows, :])
+        total = transfer_of(u, v, w) * (count[rows, :] * temp - later[rows, :])
         fresh[3] = fresh[3] - WALL_WEIGHT * total
         for c in range(NV):
-            ob[c, x] = fresh[c]
+            out_state[c, x] = fresh[c]
         return 0
 
-    def second_half(part):
-        lax.fori_loop(part * 16, part * 16 + 16, second, 0, unroll=2)
-        out = pltpu.make_async_copy(
-            ob.at[:, pl.ds(part * 16, 16)],
-            out_state.at[:, pl.ds(part * 16, 16)],
-            out_sem.at[part],
-        )
-        out.start()
-        outs.append(out)
-
-    second_half(0)
-
+    lax.fori_loop(0, XL, second, 0, unroll=4)
+    flux_arrivals()
+    out_flux[...] = frecv[...]
+    for copy in wall_copies + precursor_copies + halos_0 + halos_1 + flux_copies:
+        copy.wait_send()
+
+
+def finish(fluid, flux, wall, out_state, out_wall, wv, fv, load_sem, out_sem):
+    loads = [
+        pltpu.make_async_copy(flux, fv, load_sem.at[0]),
+        pltpu.make_async_copy(wall, wv, load_sem.at[1]),
+    ]
+    outs = [pltpu.make_async_copy(fluid.at[c], out_state.at[c], out_sem.at[c]) for c in range(NV)]
+    for copy in loads + outs:
+        copy.start()
+    for load in loads:
+        load.wait()
     layer = iota((LAYERS, 128), 0)
 
     def conduct(temps, flux_row):
@@ -591,46 +615,35 @@
         from_below = jnp.where(layer == 0, flux_row, -pltpu.roll(flow, 1, 0))
         return temps + SOLID_STEP * (flow + from_below)
 
-    flux_arrivals()
-
     def wall_tiles(t, _):
-        cols = [pl.ds(pl.multiple_of((t * 8 + i) * 128, 128), 128) for i in range(8)]
+        cols = [pl.ds(pl.multiple_of((t * 16 + i) * 128, 128), 128) for i in range(16)]
         temps = [wv[:, col] for col in cols]
         for step in range(2):
-            rows = [frecv[step, pl.ds(t * 8 + i, 1), :] for i in range(8)]
+            rows = [fv[step, pl.ds(t * 16 + i, 1), :] for i in range(16)]
             temps = [conduct(temp, flux_row) for temp, flux_row in zip(temps, rows)]
         for col, temp in zip(cols, temps):
             wv[:, col] = temp
         return 0
 
-    lax.fori_loop(0, COLUMNS // 1024, wall_tiles, 0)
-    out = pltpu.make_async_copy(wv, out_wall, out_sem.at[2])
+    lax.fori_loop(0, COLUMNS // 2048, wall_tiles, 0)
+    out = pltpu.make_async_copy(wv, out_wall, out_sem.at[4])
     out.start()
-    outs.append(out)
-
-    second_half(1)
-    for copy in wall_copies + precursor_copies + halos_0 + halos_1 + flux_copies:
-        copy.wait_send()
-    for out in outs:
-        out.wait()
+    for copy in outs + [out]:
+        copy.wait()
 
 
 def local(state, precursor, inlet_map, face_cell, face_owner, wall_temp):
     any_space = pl.BlockSpec(memory_space=pl.ANY)
     vmem = pltpu.VMEM
     dma = pltpu.SemaphoreType.DMA
-    new_state, new_wall = pl.pallas_call(
+    fluid, flux = pl.pallas_call(
         kernel,
-        out_shape=(
-            jax.ShapeDtypeStruct((NV, XL, CY, CZ), F32),
-            jax.ShapeDtypeStruct((LAYERS, COLUMNS), F32),
-        ),
+        out_shape=(vmem((NV, XL, CY, CZ), F32), vmem((2, 64, 128), F32)),
         in_specs=[any_space] * 6,
-        out_specs=(any_space, any_space),
+        out_specs=(pl.BlockSpec(memory_space=vmem),) * 2,
         scratch_shapes=[
             vmem((NV, XL + 2, PITCH, CZ), F32),
             vmem((NV, XL + 2, PITCH, CZ), F32),
-            vmem((NV, XL, CY, CZ), F32),
             vmem((LAYERS, COLUMNS), F32),
             vmem((2, NV, CAP), BF16),
             vmem((CY, CZ), I32),
@@ -651,6 +664,8 @@
             vmem((256, CY * CZ), BF16),
             vmem((32, FACES), BF16),
             vmem((640, FACES), BF16),
+            vmem((128, FACES), BF16),
+            vmem((4, 512, 128), BF16),
             vmem((4, 512, 128), BF16),
             vmem((128, 256), BF16),
             vmem((ROWS, 128), F32),
@@ -667,10 +682,14 @@
             vmem((512, 128), F32),
             vmem((512, 128), F32),
             vmem((512, 128), F32),
-            vmem((ROWS, 128), F32),
-            vmem((ROWS, 128), F32),
-            vmem((ROWS, 128), F32),
-            vmem((ROWS, 128), F32),
+            vmem((512, 128), F32),
+            vmem((ROWS, 128), F32),
+            vmem((ROWS, 128), F32),
+            vmem((ROWS, 128), F32),
+            vmem((ROWS, 128), F32),
+            vmem((ROWS, 128), F32),
+            vmem((256, CHUNK), F32),
+            vmem((256, CHUNK), F32),
             dma((6,)),
             dma((N_INFLOW - 1,)),
             dma((N_INFLOW - 1,)),
@@ -680,10 +699,9 @@
             dma((2, 2, 2)),
             dma((N_SOLID - 1,)),
             dma((N_SOLID - 1,)),
-            dma((3,)),
         ],
         compiler_params=pltpu.CompilerParams(
-            collective_id=0, has_side_effects=True, vmem_limit_bytes=62 * 1024 * 1024
+            collective_id=0, has_side_effects=True, vmem_limit_bytes=60 * 1024 * 1024
         ),
         name="manifold_step",
     )(
@@ -694,6 +712,23 @@
         face_owner.reshape(ROWS, 128),
         wall_temp[0, 0, 0],
     )
+    new_state, new_wall = pl.pallas_call(
+        finish,
+        out_shape=(
+            jax.ShapeDtypeStruct((NV, XL, CY, CZ), F32),
+            jax.ShapeDtypeStruct((LAYERS, COLUMNS), F32),
+        ),
+        in_specs=[any_space] * 3,
+        out_specs=(any_space, any_space),
+        scratch_shapes=[
+            vmem((LAYERS, COLUMNS), F32),
+            vmem((2, 64, 128), F32),
+            dma((2,)),
+            dma((1 + NV,)),
+        ],
+        compiler_params=pltpu.CompilerParams(vmem_limit_bytes=8 * 1024 * 1024),
+        name="finish",
+    )(fluid, flux, wall_temp[0, 0, 0])
     return new_state[None], new_wall[None, None, None]
 
 

time: 35.4 us -> 29.6 us (0.84); the launches traced: 35 us -> 29.5 us
  local copies, waits for them, and re-layouts: 3.03 us -> 0.01 us
  Pallas kernels: 31.3 us -> 28.9 us
    unnamed x4 -> x2, local copies, waits for them, and re-layouts: 3.03 us -> 0.01 us
    pallas_call x1 -> x2, Pallas kernels: 31.3 us -> 28.9 us  [the longest x1 27.6 us: local(): pl.pallas_call(kernel, out_shape=(vmem((NV, XL, CY, CZ), F32), vmem((2, 6...]
where the time goes in v3:
time: 29.6 us; the launch traced here: 29.5 us
  Pallas kernels  28.9 us (98%)
  between operations  0.66 us (2%)
    pallas_call x1, Pallas kernels, local(): pl.pallas_call(kernel, out_shape=(vmem((NV, XL, CY, CZ), F32), vmem((2, 6...  27.6 us
    pallas_call x1, Pallas kernels, local(): pl.pallas_call(finish, out_shape=(jax.ShapeDtypeStruct((NV, XL, CY, CZ),...  1.29 us

profile of v3, /device:TPU:1, one launch (start us, length us, event | category | flops | bytes accessed | tf_op | source)
XLA Modules:
  0.0 29.5 jit_solution(4803249885966458401)
XLA Ops:
  0.6 0.0 copy-start
  0.6 27.6 %manifold_step.1 = (f32[4,32,16,128]{3,2,1,0:T(8,128)S(1)}, f32[2,64,128]{2,1,0:T(8,128)S(1)}) custom-call(f32[4,32,16,128]{3,2,1,0:T(8,128)} %bitcast.10, bf16[2,4,2048]{2,1,0:T(4,128)(2,1)} %bitcast.11, s32[16,128]{1,0:T(8,128)} %bitcast.14, s32[32,128]{1,0:T(8,128)} %bitcast.12, s32[32,128]{1,0:T(8,128)} %bitcast.13, f32[8,8192]{1,0:T(8,128)} %bitcast.8), custom_call_target="tpu_custom_call" | custom-call | tf_op jit(solution)/shard_map/manifold_step/pallas_call | solution.py:639
  28.2 0.0 copy-done
  28.2 1.3 %finish.1 = (f32[4,32,16,128]{3,2,1,0:T(8,128)}, f32[8,8192]{1,0:T(8,128)}) custom-call(f32[4,32,16,128]{3,2,1,0:T(8,128)S(1)} %get-tuple-element.6.fluid, f32[2,64,128]{2,1,0:T(8,128)S(1)} %get-tuple-element.7.flux, f32[8,8192]{1,0:T(8,128)S(1)} %bitcast.9), custom_call_target="tpu_custom_call" | custom-call | tf_op jit(solution)/shard_map/finish/pallas_call | solution.py:715
Async XLA Ops:
  0.6 27.6 %copy-start = (f32[1,1,1,8,8192]{4,3,2,1,0:T(8,128)S(1)}, f32[1,1,1,8,8192]{4,3,2,1,0:T(8,128)}, u32[]{:S(2)}) copy-start(f32[1,1,1,8,8192]{4,3,2,1,0:T(8,128)} %param.11) | copy-start | bytes 786436

commit v4 on v3

--- a/solution.py
+++ b/solution.py
@@ -353,7 +353,7 @@
             one_hots_of_inlet(n * 2 + i)
         return packed
 
-    packed = lax.fori_loop(0, XL // 4, prepare, (zero_plane, zero_plane))
+    packed = lax.fori_loop(0, XL // 4, prepare, (zero_plane, zero_plane), unroll=4)
     hz_send[0, 0] = packed[0]
     hz_send[0, 1] = packed[1]
     halos_0 = halo_copies(0)
@@ -389,7 +389,7 @@
             sample_pick(2 * m + 1, found_1)
             return carry
 
-        return lax.fori_loop(0, CHUNKS // 2, two, carry)
+        return lax.fori_loop(0, CHUNKS // 2, two, carry, unroll=CHUNKS // 2 if step == 0 else 2)
 
     own = pl.multiple_of(so * 32, 32)
     wrecv[pl.ds(own, 32)] = wsend[pl.ds(own, 32)]
@@ -474,7 +474,7 @@
                 )
             return 0
 
-        lax.fori_loop(0, XL, rows_of, 0, unroll=8)
+        lax.fori_loop(0, XL, rows_of, 0, unroll=32)
         merged = []
         for part in range(2):
             low = jnp.where(inf > 0, pltpu.roll(hz_recv[step, 0, part], 1, 1), 0.0)
@@ -584,23 +584,17 @@
             out_state[c, x] = fresh[c]
         return 0
 
-    lax.fori_loop(0, XL, second, 0, unroll=4)
+    lax.fori_loop(0, XL, second, 0, unroll=16)
     flux_arrivals()
     out_flux[...] = frecv[...]
     for copy in wall_copies + precursor_copies + halos_0 + halos_1 + flux_copies:
         copy.wait_send()
 
 
-def finish(fluid, flux, wall, out_state, out_wall, wv, fv, load_sem, out_sem):
-    loads = [
-        pltpu.make_async_copy(flux, fv, load_sem.at[0]),
-        pltpu.make_async_copy(wall, wv, load_sem.at[1]),
-    ]
+def finish(fluid, fv, wall, out_state, out_wall, wv, out_sem):
     outs = [pltpu.make_async_copy(fluid.at[c], out_state.at[c], out_sem.at[c]) for c in range(NV)]
-    for copy in loads + outs:
+    for copy in outs:
         copy.start()
-    for load in loads:
-        load.wait()
     layer = iota((LAYERS, 128), 0)
 
     def conduct(temps, flux_row):
@@ -615,20 +609,18 @@
         from_below = jnp.where(layer == 0, flux_row, -pltpu.roll(flow, 1, 0))
         return temps + SOLID_STEP * (flow + from_below)
 
-    def wall_tiles(t, _):
-        cols = [pl.ds(pl.multiple_of((t * 16 + i) * 128, 128), 128) for i in range(16)]
-        temps = [wv[:, col] for col in cols]
+    for part in range(4):
+        cols = [slice((part * 16 + i) * 128, (part * 16 + i + 1) * 128) for i in range(16)]
+        temps = [wall[:, col] for col in cols]
         for step in range(2):
-            rows = [fv[step, pl.ds(t * 16 + i, 1), :] for i in range(16)]
+            rows = [fv[step, part * 16 + i : part * 16 + i + 1, :] for i in range(16)]
             temps = [conduct(temp, flux_row) for temp, flux_row in zip(temps, rows)]
         for col, temp in zip(cols, temps):
             wv[:, col] = temp
-        return 0
-
-    lax.fori_loop(0, COLUMNS // 2048, wall_tiles, 0)
-    out = pltpu.make_async_copy(wv, out_wall, out_sem.at[4])
-    out.start()
-    for copy in outs + [out]:
+        span = slice(part * 2048, (part + 1) * 2048)
+        outs.append(pltpu.make_async_copy(wv.at[:, span], out_wall.at[:, span], out_sem.at[NV + part]))
+        outs[-1].start()
+    for copy in outs:
         copy.wait()
 
 
@@ -718,13 +710,11 @@
             jax.ShapeDtypeStruct((NV, XL, CY, CZ), F32),
             jax.ShapeDtypeStruct((LAYERS, COLUMNS), F32),
         ),
-        in_specs=[any_space] * 3,
+        in_specs=[any_space] + [pl.BlockSpec(memory_space=vmem)] * 2,
         out_specs=(any_space, any_space),
         scratch_shapes=[
             vmem((LAYERS, COLUMNS), F32),
-            vmem((2, 64, 128), F32),
-            dma((2,)),
-            dma((1 + NV,)),
+            dma((2 * NV,)),
         ],
         compiler_params=pltpu.CompilerParams(vmem_limit_bytes=8 * 1024 * 1024),
         name="finish",

time: 29.6 us -> 28.6 us (0.966)
  Pallas kernels: 28.9 us -> 27.9 us
    pallas_call x1, Pallas kernels: 27.6 us -> 26.8 us  [local(): pl.pallas_call(kernel, out_shape=(vmem((NV, XL, CY, CZ), F32), vmem((2, 6...]
where the time goes in v4:
time: 28.6 us; the launch traced here: 28.5 us
  Pallas kernels  27.9 us (98%)
  between operations  0.66 us (2%)
    pallas_call x1, Pallas kernels, local(): pl.pallas_call(kernel, out_shape=(vmem((NV, XL, CY, CZ), F32), vmem((2, 6...  26.8 us
    pallas_call x1, Pallas kernels, local(): pl.pallas_call(finish, out_shape=(jax.ShapeDtypeStruct((NV, XL, CY, CZ),...  1.11 us

profile of v4, /device:TPU:1, one launch (start us, length us, event | category | flops | bytes accessed | tf_op | source)
XLA Modules:
  0.0 28.5 jit_solution(9195584038975352850)
XLA Ops:
  0.6 0.0 copy-start
  0.6 26.8 %manifold_step.1 = (f32[4,32,16,128]{3,2,1,0:T(8,128)S(1)}, f32[2,64,128]{2,1,0:T(8,128)S(1)}) custom-call(f32[4,32,16,128]{3,2,1,0:T(8,128)} %bitcast.10, bf16[2,4,2048]{2,1,0:T(4,128)(2,1)} %bitcast.11, s32[16,128]{1,0:T(8,128)} %bitcast.14, s32[32,128]{1,0:T(8,128)} %bitcast.12, s32[32,128]{1,0:T(8,128)} %bitcast.13, f32[8,8192]{1,0:T(8,128)} %bitcast.8), custom_call_target="tpu_custom_call" | custom-call | tf_op jit(solution)/shard_map/manifold_step/pallas_call | solution.py:631
  27.4 0.0 copy-done
  27.4 1.1 %finish.1 = (f32[4,32,16,128]{3,2,1,0:T(8,128)}, f32[8,8192]{1,0:T(8,128)}) custom-call(f32[4,32,16,128]{3,2,1,0:T(8,128)S(1)} %get-tuple-element.6.fluid, f32[2,64,128]{2,1,0:T(8,128)S(1)} %get-tuple-element.7.fv, f32[8,8192]{1,0:T(8,128)S(1)} %bitcast.9), custom_call_target="tpu_custom_call" | custom-call | tf_op jit(solution)/shard_map/finish/pallas_call | solution.py:707
Async XLA Ops:
  0.6 26.8 %copy-start = (f32[1,1,1,8,8192]{4,3,2,1,0:T(8,128)S(1)}, f32[1,1,1,8,8192]{4,3,2,1,0:T(8,128)}, u32[]{:S(2)}) copy-start(f32[1,1,1,8,8192]{4,3,2,1,0:T(8,128)} %param.11) | copy-start | bytes 786436

commit v5 on v4

--- a/solution.py
+++ b/solution.py
@@ -130,8 +130,6 @@
         pltpu.make_async_copy(imap, imv, load_sem.at[5]),
         pltpu.make_async_copy(state, q0.at[:, pl.ds(1, XL), pl.ds(TOP, CY)], load_sem.at[2]),
     ]
-    for load in loads:
-        load.start()
 
     barrier = pltpu.get_barrier_semaphore()
 
@@ -144,6 +142,9 @@
         greet({"fluid": (fl + d) & (N_FLUID - 1)})
     for d in range(1, N_SOLID):
         greet({"solid": (so + d) & (N_SOLID - 1)})
+
+    for load in loads:
+        load.start()
 
     lane = iota((CY, CZ), 1)
 
@@ -246,35 +247,6 @@
                 device_id={"solid": came},
                 device_id_type=MESH,
             ).wait_recv()
-
-    pl.semaphore_wait(barrier, (N_INFLOW - 1) + 2 + (N_SOLID - 1))
-    for copy in wall_copies + precursor_copies:
-        copy.start()
-
-    def pair_of(c, x):
-        return (c % 2) * XL + x
-
-    def keep_edges(step, x, values, packed):
-        packed = list(packed)
-        for c in range(NV):
-            k = c * XL + x
-            hy_send[step, 0, pl.ds(k, 1), :] = values[c][0:1]
-            hy_send[step, 1, pl.ds(k, 1), :] = values[c][CY - 1 : CY]
-            j = pair_of(c, x)
-            moved = pltpu.roll(values[c], 2 * j + 1, 1)
-            packed[c // 2] = jnp.where(lax.shift_right_logical(lane, 1) == j, moved, packed[c // 2])
-        return tuple(packed)
-
-    zero_plane = jnp.zeros((CY, CZ), F32)
-    lhs = (lhs_0, lhs_1)
-
-    def keep_sample_plane(step, x, u, v, w, temp):
-        (a_high, a_low), (b_high, b_low) = split(transfer_of(u, v, w)), split(temp)
-        parts = (a_high, b_high, a_low, b_low)
-        quarter = lax.shift_right_logical(x, 3)
-        at = pl.multiple_of((x & 7) * CY, CY)
-        for i, part in enumerate(parts):
-            lhs[step][quarter, pl.ds(i * 128 + at, CY), :] = part
 
     for load in loads[2:5]:
         load.wait()
@@ -306,6 +278,35 @@
     zi[...] = (relative & 127).astype(F32)
     hi_in[...] = lax.shift_right_logical(hi, 6).astype(F32)
     ri[...] = hi & 63
+
+    pl.semaphore_wait(barrier, (N_INFLOW - 1) + 2 + (N_SOLID - 1))
+    for copy in wall_copies + precursor_copies:
+        copy.start()
+
+    def pair_of(c, x):
+        return (c % 2) * XL + x
+
+    def keep_edges(step, x, values, packed):
+        packed = list(packed)
+        for c in range(NV):
+            k = c * XL + x
+            hy_send[step, 0, pl.ds(k, 1), :] = values[c][0:1]
+            hy_send[step, 1, pl.ds(k, 1), :] = values[c][CY - 1 : CY]
+            j = pair_of(c, x)
+            moved = pltpu.roll(values[c], 2 * j + 1, 1)
+            packed[c // 2] = jnp.where(lax.shift_right_logical(lane, 1) == j, moved, packed[c // 2])
+        return tuple(packed)
+
+    zero_plane = jnp.zeros((CY, CZ), F32)
+    lhs = (lhs_0, lhs_1)
+
+    def keep_sample_plane(step, x, u, v, w, temp):
+        (a_high, a_low), (b_high, b_low) = split(transfer_of(u, v, w)), split(temp)
+        parts = (a_high, b_high, a_low, b_low)
+        quarter = lax.shift_right_logical(x, 3)
+        at = pl.multiple_of((x & 7) * CY, CY)
+        for i, part in enumerate(parts):
+            lhs[step][quarter, pl.ds(i * 128 + at, CY), :] = part
 
     steps_128 = iota((128, 128), 0).astype(F32).astype(BF16)
     one, zero = jnp.ones((), BF16), jnp.zeros((), BF16)

time: 28.6 us -> 28.3 us (0.990)
  Pallas kernels: 27.9 us -> 27.6 us
    pallas_call x1, Pallas kernels: 26.8 us -> 26.4 us  [local(): pl.pallas_call(kernel, out_shape=(vmem((NV, XL, CY, CZ), F32), vmem((2, 6...]
where the time goes in v5:
time: 28.3 us; the launch traced here: 28.2 us
  Pallas kernels  27.6 us (98%)
  between operations  0.66 us (2%)
    pallas_call x1, Pallas kernels, local(): pl.pallas_call(kernel, out_shape=(vmem((NV, XL, CY, CZ), F32), vmem((2, 6...  26.4 us
    pallas_call x1, Pallas kernels, local(): pl.pallas_call(finish, out_shape=(jax.ShapeDtypeStruct((NV, XL, CY, CZ),...  1.11 us

profile of v5, /device:TPU:1, one launch (start us, length us, event | category | flops | bytes accessed | tf_op | source)
XLA Modules:
  0.0 28.2 jit_solution(15404187776571248796)
XLA Ops:
  0.6 0.0 copy-start
  0.6 26.4 %manifold_step.1 = (f32[4,32,16,128]{3,2,1,0:T(8,128)S(1)}, f32[2,64,128]{2,1,0:T(8,128)S(1)}) custom-call(f32[4,32,16,128]{3,2,1,0:T(8,128)} %bitcast.10, bf16[2,4,2048]{2,1,0:T(4,128)(2,1)} %bitcast.11, s32[16,128]{1,0:T(8,128)} %bitcast.14, s32[32,128]{1,0:T(8,128)} %bitcast.12, s32[32,128]{1,0:T(8,128)} %bitcast.13, f32[8,8192]{1,0:T(8,128)} %bitcast.8), custom_call_target="tpu_custom_call" | custom-call | tf_op jit(solution)/shard_map/manifold_step/pallas_call | solution.py:632
  27.1 0.0 copy-done
  27.1 1.1 %finish.1 = (f32[4,32,16,128]{3,2,1,0:T(8,128)}, f32[8,8192]{1,0:T(8,128)}) custom-call(f32[4,32,16,128]{3,2,1,0:T(8,128)S(1)} %get-tuple-element.6.fluid, f32[2,64,128]{2,1,0:T(8,128)S(1)} %get-tuple-element.7.fv, f32[8,8192]{1,0:T(8,128)S(1)} %bitcast.9), custom_call_target="tpu_custom_call" | custom-call | tf_op jit(solution)/shard_map/finish/pallas_call | solution.py:708
Async XLA Ops:
  0.6 26.5 %copy-start = (f32[1,1,1,8,8192]{4,3,2,1,0:T(8,128)S(1)}, f32[1,1,1,8,8192]{4,3,2,1,0:T(8,128)}, u32[]{:S(2)}) copy-start(f32[1,1,1,8,8192]{4,3,2,1,0:T(8,128)} %param.11) | copy-start | bytes 786436

commit v6 on v5

--- a/solution.py
+++ b/solution.py
@@ -279,6 +279,42 @@
     hi_in[...] = lax.shift_right_logical(hi, 6).astype(F32)
     ri[...] = hi & 63
 
+    steps_128 = iota((128, 128), 0).astype(F32).astype(BF16)
+    one, zero = jnp.ones((), BF16), jnp.zeros((), BF16)
+
+    def wide(row_values, blocks):
+        tile = jnp.broadcast_to(row_values, (16, 128)).astype(BF16)
+        return jnp.concatenate([tile] * blocks, axis=0) if blocks > 1 else tile
+
+    def hot(row_values, blocks):
+        return jnp.where(steps_128[: blocks * 16] == wide(row_values, blocks), one, zero)
+
+    def marked(row_values, value, blocks):
+        return wide(jnp.where(row_values == value, 1.0, 0.0), blocks)
+
+    def lanes_of(j):
+        return pl.ds(pl.multiple_of(j * 128, 128), 128)
+
+    def one_hots_of_faces(j):
+        at, cols = pl.ds(j, 1), lanes_of(j)
+        base, quarter = hot(zf[at, :], 8), qf[at, :]
+        for part in range(4):
+            oh_cell[part * 128 : (part + 1) * 128, cols] = base * marked(quarter, float(part), 8)
+        vm[0:128, cols] = hot(rf[at, :], 8)
+        base, half = hot(lf[at, :], 8), hf[at, :]
+        for part in range(2):
+            oh_slot[part * 128 : (part + 1) * 128, cols] = base * marked(half, float(part), 8)
+        oh_srow[:, cols] = hot(sf[at, :], 2)
+
+    def one_hots_of_inlet(j):
+        at, cols = slice(j, j + 1), slice(j * 128, (j + 1) * 128)
+        base, half = hot(zi[at, :], 8), hi_in[at, :]
+        for part in range(2):
+            oh_in[part * 128 : (part + 1) * 128, cols] = base * marked(half, float(part), 8)
+
+    for j in range(CY):
+        one_hots_of_inlet(j)
+
     pl.semaphore_wait(barrier, (N_INFLOW - 1) + 2 + (N_SOLID - 1))
     for copy in wall_copies + precursor_copies:
         copy.start()
@@ -308,39 +344,6 @@
         for i, part in enumerate(parts):
             lhs[step][quarter, pl.ds(i * 128 + at, CY), :] = part
 
-    steps_128 = iota((128, 128), 0).astype(F32).astype(BF16)
-    one, zero = jnp.ones((), BF16), jnp.zeros((), BF16)
-
-    def wide(row_values, blocks):
-        tile = jnp.broadcast_to(row_values, (16, 128)).astype(BF16)
-        return jnp.concatenate([tile] * blocks, axis=0) if blocks > 1 else tile
-
-    def hot(row_values, blocks):
-        return jnp.where(steps_128[: blocks * 16] == wide(row_values, blocks), one, zero)
-
-    def marked(row_values, value, blocks):
-        return wide(jnp.where(row_values == value, 1.0, 0.0), blocks)
-
-    def lanes_of(j):
-        return pl.ds(pl.multiple_of(j * 128, 128), 128)
-
-    def one_hots_of_faces(j):
-        at, cols = pl.ds(j, 1), lanes_of(j)
-        base, quarter = hot(zf[at, :], 8), qf[at, :]
-        for part in range(4):
-            oh_cell[part * 128 : (part + 1) * 128, cols] = base * marked(quarter, float(part), 8)
-        vm[0:128, cols] = hot(rf[at, :], 8)
-        base, half = hot(lf[at, :], 8), hf[at, :]
-        for part in range(2):
-            oh_slot[part * 128 : (part + 1) * 128, cols] = base * marked(half, float(part), 8)
-        oh_srow[:, cols] = hot(sf[at, :], 2)
-
-    def one_hots_of_inlet(j):
-        at, cols = pl.ds(j, 1), lanes_of(j)
-        base, half = hot(zi[at, :], 8), hi_in[at, :]
-        for part in range(2):
-            oh_in[part * 128 : (part + 1) * 128, cols] = base * marked(half, float(part), 8)
-
     loads[5].wait()
 
     def prepare(n, packed):
@@ -350,8 +353,6 @@
             keep_sample_plane(0, x, *values)
             packed = keep_edges(0, x, values, packed)
             one_hots_of_faces(n * 4 + i)
-        for i in range(2):
-            one_hots_of_inlet(n * 2 + i)
         return packed
 
     packed = lax.fori_loop(0, XL // 4, prepare, (zero_plane, zero_plane), unroll=4)

time: 28.3 us -> 28 us (0.989)
  Pallas kernels: 27.6 us -> 27.3 us
    pallas_call x1, Pallas kernels: 26.4 us -> 26.1 us  [local(): pl.pallas_call(kernel, out_shape=(vmem((NV, XL, CY, CZ), F32), vmem((2, 6...]
where the time goes in v6:
time: 28 us; the launch traced here: 27.9 us
  Pallas kernels  27.3 us (98%)
  between operations  0.66 us (2%)
    pallas_call x1, Pallas kernels, local(): pl.pallas_call(kernel, out_shape=(vmem((NV, XL, CY, CZ), F32), vmem((2, 6...  26.1 us
    pallas_call x1, Pallas kernels, local(): pl.pallas_call(finish, out_shape=(jax.ShapeDtypeStruct((NV, XL, CY, CZ),...  1.11 us

profile of v6, /device:TPU:1, one launch (start us, length us, event | category | flops | bytes accessed | tf_op | source)
XLA Modules:
  0.0 27.9 jit_solution(5412912166736188883)
XLA Ops:
  0.6 0.0 copy-start
  0.6 26.1 %manifold_step.1 = (f32[4,32,16,128]{3,2,1,0:T(8,128)S(1)}, f32[2,64,128]{2,1,0:T(8,128)S(1)}) custom-call(f32[4,32,16,128]{3,2,1,0:T(8,128)} %bitcast.10, bf16[2,4,2048]{2,1,0:T(4,128)(2,1)} %bitcast.11, s32[16,128]{1,0:T(8,128)} %bitcast.14, s32[32,128]{1,0:T(8,128)} %bitcast.12, s32[32,128]{1,0:T(8,128)} %bitcast.13, f32[8,8192]{1,0:T(8,128)} %bitcast.8), custom_call_target="tpu_custom_call" | custom-call | tf_op jit(solution)/shard_map/manifold_step/pallas_call | solution.py:633
  26.8 0.0 copy-done
  26.8 1.1 %finish.1 = (f32[4,32,16,128]{3,2,1,0:T(8,128)}, f32[8,8192]{1,0:T(8,128)}) custom-call(f32[4,32,16,128]{3,2,1,0:T(8,128)S(1)} %get-tuple-element.6.fluid, f32[2,64,128]{2,1,0:T(8,128)S(1)} %get-tuple-element.7.fv, f32[8,8192]{1,0:T(8,128)S(1)} %bitcast.9), custom_call_target="tpu_custom_call" | custom-call | tf_op jit(solution)/shard_map/finish/pallas_call | solution.py:709
Async XLA Ops:
  0.6 26.2 %copy-start = (f32[1,1,1,8,8192]{4,3,2,1,0:T(8,128)S(1)}, f32[1,1,1,8,8192]{4,3,2,1,0:T(8,128)}, u32[]{:S(2)}) copy-start(f32[1,1,1,8,8192]{4,3,2,1,0:T(8,128)} %param.11) | copy-start | bytes 786436
